TPU v7x, 512 devices: a whole 4x8x8 slice. The times are simulated.
512 devices in a mesh: dp: 128 (over z, y, core), mp: 4 (over x).
Axes of the slice: x: 4, y: 8, z: 8, core: 2. Of those that a mesh axis runs over, the one named last changes fastest.
Arguments:
- images: bfloat16 [32768, 1664], P('dp'), may hold values from -6 to 6
- attn_gain: float32 [1664], replicated, may hold values from 0.25 to 1.75
- qkv_weight: bfloat16 [3, 1664, 1664], P(None, 'dp', 'mp'), may hold values from -12 to 12
- proj_weight: bfloat16 [1664, 1664], P('mp', 'dp'), may hold values from -0.15625 to 0.15625
- mlp_gain: float32 [1664], replicated, may hold values from 0.25 to 1.75
- expert_in: bfloat16 [1664, 262144], P(None, ('dp', 'mp')), may hold values from -0.15625 to 0.15625
- expert_out: bfloat16 [262144, 1664], P(('dp', 'mp')), may hold values from -0.0625 to 0.0625
- gate_values: bfloat16 [32768, 2], P('dp'), may hold values from 0.25 to 1, as said below
- expert_ids: int32 [32768, 2], P('dp'), may hold values from 0 to 31, as said below
- kept_patches: int32 [128, 32, 8], P('dp'), may hold values from 0 to 255, as said below
- kept_counts: int32 [128, 32], P('dp'), may hold values from 0 to 8, as said below
Outputs:
- block_out: bfloat16 [32768, 1664], P(('dp', 'mp'))
Inputs may be any that keep to these rules, and one draw needn't show every extreme that they name: `expert_ids`: each token names 2 different experts. `kept_patches`: for image i and expert e, slots 0 to kept_counts[i, e] - 1 hold different patches of image i whose expert_ids name e, in order of priority: patches ordered by their largest gate value, larger first, ties by lower patch number; every patch naming e that is not listed there has lower priority than all listed ones and was dropped because those slots are full; the later slots are padding with patch numbers of that image. `kept_counts`: the number of valid slots; it equals 8 wherever 8 or more patches of the image name the expert, else the number of such patches. `gate_values`: each patch's first gate value is larger than its second.
All inputs are finite; a program needn't handle non-finite values.
Results may differ from a plain program's by a relative error of at most 0.015.
Values may be sent and summed in bfloat16 or wider, within the bound.
A program may use at most 64 MiB of HBM per device.

v0:
```python
import jax
import jax.numpy as jnp
from jax import lax
from jax.sharding import PartitionSpec as P

EXPERTS = 32
PATCHES = 256
HEAD_DIM = 104


def layer_norm(values, norm_gain):
    center = values - jnp.mean(values, axis=-1, keepdims=True)
    spread = jnp.mean(center * center, axis=-1, keepdims=True)
    return center * lax.rsqrt(spread + 1e-06) * norm_gain


def gelu_tanh(values):
    return (
        0.5
        * values
        * (1.0 + jnp.tanh(0.7978845608028654 * (values + 0.044715 * values * values * values)))
    )


def attend(query_rows, key_rows, value_rows, image_count):
    local_cols = query_rows.shape[1]
    local_heads = local_cols // HEAD_DIM

    def shaped(block):
        return block.reshape(image_count, PATCHES, local_heads, HEAD_DIM)

    scores = jnp.einsum(
        "iphd,iqhd->ihpq", shaped(query_rows), shaped(key_rows), preferred_element_type=jnp.float32
    ) * HEAD_DIM ** (-0.5)
    probs = jax.nn.softmax(scores, axis=-1).astype(jnp.bfloat16)
    mixed = jnp.einsum(
        "ihpq,iqhd->iphd", probs, shaped(value_rows), preferred_element_type=jnp.float32
    )
    return mixed.astype(jnp.bfloat16).reshape(image_count * PATCHES, local_cols)


def on_device(
    images,
    attn_gain,
    qkv_weight,
    proj_weight,
    mlp_gain,
    expert_in,
    expert_out,
    gate_values,
    expert_ids,
    kept_patches,
    kept_counts,
):
    row_count = images.shape[0]
    model_width = images.shape[1]
    image_count = row_count // PATCHES
    dp_size = lax.axis_size("dp")
    mp_size = lax.axis_size("mp")
    inputs = images.astype(jnp.float32)
    normed = layer_norm(inputs, attn_gain).astype(jnp.bfloat16)
    full_qkv, full_proj = (
        lax.all_gather(qkv_weight, "dp", axis=1, tiled=True),
        lax.all_gather(proj_weight, "dp", axis=1, tiled=True),
    )
    projected = jnp.einsum(
        "rn,knc->krc", normed, full_qkv, preferred_element_type=jnp.float32
    ).astype(jnp.bfloat16)
    heads_out = attend(projected[0], projected[1], projected[2], image_count)
    attn_part = jnp.dot(heads_out, full_proj, preferred_element_type=jnp.float32)
    share = row_count // mp_size
    share_start = lax.axis_index("mp") * share
    residual = inputs + lax.psum(attn_part.astype(jnp.bfloat16), "mp").astype(jnp.float32)
    routed = layer_norm(residual, mlp_gain).astype(jnp.bfloat16)
    residual_own = lax.dynamic_slice_in_dim(residual, share_start, share, 0)
    slot_count = kept_patches.shape[2]
    group_size = dp_size * mp_size // EXPERTS
    targets = (jnp.arange(dp_size, dtype=jnp.int32) * mp_size + lax.axis_index("mp")) // group_size
    kept_dest = jnp.take(kept_patches, targets, axis=1)
    offsets = (jnp.arange(image_count, dtype=jnp.int32) * PATCHES)[:, None, None]
    slot_rows = jnp.transpose(kept_dest + offsets, (1, 0, 2)).reshape(-1)
    per_dest = image_count * slot_count
    outgoing = jnp.take(routed, slot_rows, axis=0).reshape(dp_size, per_dest, model_width)
    arrived = lax.all_to_all(outgoing, "dp", split_axis=0, concat_axis=0, tiled=True)
    flat_rows = arrived.reshape(-1, model_width)
    hidden = gelu_tanh(jnp.dot(flat_rows, expert_in, preferred_element_type=jnp.float32)).astype(
        jnp.bfloat16
    )
    partial_value = jnp.dot(hidden, expert_out, preferred_element_type=jnp.float32).astype(
        jnp.bfloat16
    )
    returned = lax.all_to_all(
        partial_value.reshape(arrived.shape), "dp", split_axis=0, concat_axis=0, tiled=True
    )
    slot_expert = jnp.repeat(targets, per_dest)
    matching = jnp.take(expert_ids, slot_rows, axis=0) == slot_expert[:, None]
    slot_gate = jnp.sum(
        jnp.where(matching, jnp.take(gate_values, slot_rows, axis=0).astype(jnp.float32), 0.0),
        axis=1,
    )
    count_dest = jnp.take(kept_counts, targets, axis=1)
    usable = (
        jnp.arange(slot_count, dtype=jnp.int32)[None, None, :]
        < jnp.transpose(count_dest)[:, :, None]
    )
    slot_weight = jnp.where(usable.reshape(-1), slot_gate, 0.0).astype(jnp.bfloat16)
    placing = jnp.where(
        slot_rows[None, :] == jnp.arange(row_count, dtype=jnp.int32)[:, None],
        slot_weight[None, :],
        jnp.zeros((), jnp.bfloat16),
    )
    expert_rows = jnp.dot(
        placing, returned.reshape(-1, model_width), preferred_element_type=jnp.float32
    )
    expert_own = lax.psum_scatter(
        expert_rows.astype(jnp.bfloat16), "mp", scatter_dimension=0, tiled=True
    ).astype(jnp.float32)
    return (residual_own + expert_own).astype(jnp.bfloat16)


def solution(mesh):
    placed = (
        P("dp", None),
        P(),
        P(None, "dp", "mp"),
        P("mp", "dp"),
        P(),
        P(None, ("dp", "mp")),
        P(("dp", "mp"), None),
        P("dp", None),
        P("dp", None),
        P("dp", None, None),
        P("dp", None),
    )
    return jax.shard_map(
        on_device, mesh=mesh, in_specs=placed, out_specs=P(("dp", "mp"), None), check_vma=False
    )
```

profile of v0, /device:TPU:8, one launch (start us, length us, event | category | flops | bytes accessed | tf_op | source)
XLA Modules:
  0.0 494.3 jit_solution(7774772684742428494)
XLA Ops:
  7.3 1.5 copy.20
  9.6 1.3 convert_reduce_fusion
  11.0 1.5 fusion.18
  12.5 84.8 %all-gather.6.cloned.1.call-done = bf16[128,13,416]{2,1,0:T(8,128)(2,1)} async-done(((bf16[1,13,416]{2,1,0:T(8,128)(2,1)}), bf16[128,13,416]{2,1,0:T(8,128)(2,1)}) %all-gather.6.cloned.1.call-update) | async-done | bytes 1384464 | tf_op jit(solution)/shard_map/all_gather | solution.py:64
  97.4 4.0 reshape.321
  101.3 83.3 %all-gather.4.cloned.1.call-done = bf16[3,1664,416]{2,0,1:T(4,128)(2,1)} async-done(((bf16[3,13,416]{2,0,1:T(4,128)(2,1)}), bf16[3,1664,416]{2,0,1:T(4,128)(2,1)}) %all-gather.4.cloned.1.call-update) | async-done | bytes 4153360 | tf_op jit(solution)/shard_map/all_gather | solution.py:63
  184.7 5.4 %fusion.28 = bf16[3,256,416]{1,2,0:T(8,128)(2,1)S(1)} fusion(bf16[3,1664,416]{2,0,1:T(4,128)(2,1)} %all-gather.4.cloned.1.call-done, bf16[256,1664]{1,0:T(8,128)(2,1)S(1)} %copy-done.2, f32[1664]{0:T(1024)S(1)} %copy-done.8, f32[256]{0:T(256)S(1)} %add_rsqrt_fusion.1, f32[256]{0:T(256)S(1)} %broadcast_multiply_fusion.1), kind=kOutput, calls=%fused_computation.37 | convolution fusion | flops 1065705472 | bytes 5652992 | tf_op jit(solution)/shard_map/rn,knc->krc/dot_general | solution.py:66
  190.1 1.3 convolution_multiply_fusion
  191.9 1.9 convolution_convert_fusion.2
  193.9 3.1 convolution_convert_fusion.1
  198.1 51.8 %all-reduce.2.cloned.1.call-done = bf16[256,1664]{1,0:T(8,128)(2,1)} async-done(((bf16[256,1664]{1,0:T(8,128)(2,1)}), bf16[256,1664]{1,0:T(8,128)(2,1)}) %all-reduce.2.cloned.1.call-update) | async-done | bytes 851984 | tf_op jit(solution)/shard_map/psum | solution.py:73
  249.9 2.7 convert_add_fusion
  253.6 5.8 %gather_fusion.4 = bf16[1024,1664]{1,0:T(8,128)(2,1)} fusion(bf16[256,1664]{1,0:T(8,128)(2,1)S(1)} %multiply_convert_fusion, s32[1024]{0:T(1024)S(1)} %broadcast_clamp_fusion), kind=kCustom, calls=%fused_computation.4 | custom fusion | bytes 6819840 | tf_op jit(solution)/shard_map/jit(_take)/gather | solution.py:83
  259.4 2.4 bitcast_select_fusion
  261.8 96.4 %all_to_all.10 = bf16[128,8,1664]{2,1,0:T(8,128)(2,1)} all-to-all(bf16[128,8,1664]{2,1,0:T(8,128)(2,1)S(1)} %bitcast_select_fusion), channel_id=1, replica_groups=mesh['dp'=128,'mp'=4] {'dp'}, dimensions={0} | all-to-all | bytes 6815744 | tf_op jit(solution)/shard_map/all_to_all | solution.py:84
  358.2 7.9 %fusion.7 = bf16[128,8,1664]{2,1,0:T(8,128)(2,1)} fusion(bf16[512,1664]{1,0:T(8,128)(2,1)S(1)} %copy-done, bf16[1664,512]{1,0:T(8,128)(2,1)S(1)} %copy-done.7, bf16[128,8,1664]{2,1,0:T(8,128)(2,1)} %all_to_all.10), kind=kOutput, calls=%fused_computation.14 | convolution fusion | flops 3496083456 | bytes 10223616 | tf_op jit(solution)/shard_map/dot_general | solution.py:89
  366.1 9.7 %all-to-all-start.1 = ((bf16[128,8,1664]{2,1,0:T(8,128)(2,1)}), bf16[128,8,1664]{2,1,0:T(8,128)(2,1)}, u32[]{:S(2)}, u32[]{:S(2)}) async-start(bf16[128,8,1664]{2,1,0:T(8,128)(2,1)} %fusion.7), calls=%async_computation.1 | async-start | bytes 6815744 | tf_op jit(solution)/shard_map/all_to_all | solution.py:92
  376.2 2.8 gather_fusion.2
  379.2 3.2 gather_fusion.3
  382.6 1.2 gather_fusion.1
  384.6 73.2 %all-to-all-done.1 = bf16[128,8,1664]{2,1,0:T(8,128)(2,1)} async-done(((bf16[128,8,1664]{2,1,0:T(8,128)(2,1)}), bf16[128,8,1664]{2,1,0:T(8,128)(2,1)}, u32[]{:S(2)}, u32[]{:S(2)}) %all-to-all-start.1) | async-done | bytes 3407904 | tf_op jit(solution)/shard_map/all_to_all | solution.py:92
  457.7 4.0 fusion.8
  461.8 24.2 %reduce-scatter.2.cloned.1.call-done = bf16[64,1664]{1,0:T(8,128)(2,1)} async-done(((bf16[256,1664]{1,0:T(8,128)(2,1)}), bf16[64,1664]{1,0:T(8,128)(2,1)}) %reduce-scatter.2.cloned.1.call-update) | async-done | bytes 213008 | tf_op jit(solution)/shard_map/reduce_scatter | solution.py:115
  486.0 1.8 add_convert_fusion
  (58 shorter events, 5.8 us)
Async XLA Ops:
  6.5 351.6 %copy-start = (bf16[512,1664]{1,0:T(8,128)(2,1)S(1)}, bf16[512,1664]{1,0:T(8,128)(2,1)}, u32[]{:S(2)}) copy-start(bf16[512,1664]{1,0:T(8,128)(2,1)} %param.17) | copy-start | bytes 5111812
  6.5 90.8 %all-gather.6.cloned.1.call-start = ((), (), s32[]{:S(2)}) async-start(), calls=%async_computation.6 | async-start | bytes 2113536 | tf_op jit(solution)/shard_map/all_gather | solution.py:64
  7.3 177.4 %all-gather.4.cloned.1.call-start = ((), (), s32[]{:S(2)}) async-start(), calls=%async_computation.3 | async-start | bytes 6868992 | tf_op jit(solution)/shard_map/all_gather | solution.py:63
  8.8 241.1 %all-reduce.2.cloned.1.call-start = ((), (), s32[]{:S(2)}) async-start(), calls=%async_computation.4 | async-start | bytes 1703936 | tf_op jit(solution)/shard_map/psum | solution.py:73
  12.5 172.1 %copy-start.2 = (bf16[256,1664]{1,0:T(8,128)(2,1)S(1)}, bf16[256,1664]{1,0:T(8,128)(2,1)}, u32[]{:S(2)}) copy-start(bf16[256,1664]{1,0:T(8,128)(2,1)} %param.11) | copy-start | bytes 2555908
  12.5 172.1 %copy-start.8 = (f32[1664]{0:T(1024)S(1)}, f32[1664]{0:T(1024)}, u32[]{:S(2)}) copy-start(f32[1664]{0:T(1024)} %param.12) | copy-start | bytes 19972
  249.9 2.7 copy-start.3
  252.5 0.7 copy-start.4
  261.8 96.4 %copy-start.7 = (bf16[1664,512]{1,0:T(8,128)(2,1)S(1)}, bf16[1664,512]{1,0:T(8,128)(2,1)}, u32[]{:S(2)}) copy-start(bf16[1664,512]{1,0:T(8,128)(2,1)} %param.16) | copy-start | bytes 5111812
  366.1 10.0 %copy-start.5 = (s32[256,2]{0,1:T(2,128)S(1)}, s32[256,2]{0,1:T(2,128)}, u32[]{:S(2)}) copy-start(s32[256,2]{0,1:T(2,128)} %param.19) | copy-start | bytes 6148
  366.1 91.6 %all-to-all-start.1 = ((bf16[128,8,1664]{2,1,0:T(8,128)(2,1)}), bf16[128,8,1664]{2,1,0:T(8,128)(2,1)}, u32[]{:S(2)}, u32[]{:S(2)}) async-start(bf16[128,8,1664]{2,1,0:T(8,128)(2,1)} %fusion.7), calls=%async_computation.1 | async-start | bytes 6815744 | tf_op jit(solution)/shard_map/all_to_all | solution.py:92
  375.8 110.1 %reduce-scatter.2.cloned.1.call-start = ((), (), s32[]{:S(2)}) async-start(), calls=%async_computation.5 | async-start | bytes 1064960 | tf_op jit(solution)/shard_map/reduce_scatter | solution.py:115
  376.2 2.8 copy-start.6
  379.1 3.6 copy-start.1
Sparse Core Ops, SparseCore 0:
  10.5 86.8 all-gather.5
  100.6 84.0 all-gather.3
  197.1 52.7 all-reduce.1
  461.9 24.0 reduce-scatter.1
where the time goes:
time: 495 us; the launch traced here: 494 us
  waiting for transfers between devices  318 us (64%)
  blocking collectives  96.4 us (19%)
  matrix products  24.2 us (5%)
  local copies, waits for them, and re-layouts  21.2 us (4%)
  between operations  13.4 us (3%)
  other arithmetic  11.3 us (2%)
  starting transfers between devices  9.86 us (2%)
    all_to_all x1, blocking collectives, on_device(): lax.all_to_all(outgoing, 'dp', split_axis=0, concat_axis=0, tiled=True)  96.4 us
    all_gather x1, waiting for transfers between devices, on_device(): lax.all_gather(proj_weight, 'dp', axis=1, tiled=True)  84.8 us
    all_gather x1, waiting for transfers between devices, on_device(): lax.all_gather(qkv_weight, 'dp', axis=1, tiled=True)  83.3 us
    all_to_all x1, waiting for transfers between devices, on_device(): lax.all_to_all(partial_value.reshape(arrived.shape), 'dp', split_axis=0,...  73.2 us
    psum x1, waiting for transfers between devices, on_device(): lax.psum(attn_part.astype(jnp.bfloat16), 'mp').astype(jnp.float32)  51.8 us
    reduce_scatter x1, waiting for transfers between devices, on_device(): lax.psum_scatter(expert_rows.astype(jnp.bfloat16), 'mp', scatter_dimensio...  24.2 us
  transfers between devices with their start and end apart: 5, of which 5 were waited for; matrix products, arithmetic and copies ran while one was open for 4% of the time, Pallas kernels for 0%

commit v1 on v0

v1 whole, which is shorter than its diff:
```python
import functools

import jax
import jax.numpy as jnp
from jax import lax
from jax.experimental import pallas as pl
from jax.experimental.pallas import tpu as pltpu
from jax.sharding import PartitionSpec as P

MESH = pl.DeviceIdType.MESH
EXPERTS = 32
PATCHES = 256
HEAD_DIM = 104
HEADS_HERE = 4
D = 1664
NX, NY, NZ = 4, 8, 8
STRIP = 13
ROWS = 16
QW = 384
QP = 512
F32 = jnp.float32
BF16 = jnp.bfloat16


def place():
    dp = lax.axis_index("dp")
    return lax.axis_index("mp"), (dp // 2) % NY, dp // (2 * NY), dp % 2


def device(x, y, z, c):
    return ((z * NY + y) * 2 + c, x)


def remote(src, dst, send, recv, target):
    return pltpu.make_async_remote_copy(
        src_ref=src, dst_ref=dst, send_sem=send, recv_sem=recv, device_id=target, device_id_type=MESH
    )


def greet(partners):
    barrier = pltpu.get_barrier_semaphore()
    for partner in partners:
        pl.semaphore_signal(barrier, inc=1, device_id=partner, device_id_type=MESH)
    pl.semaphore_wait(barrier, len(partners))


def strip_pick(feature0, rows, chunk, cols):
    feature = lax.broadcasted_iota(jnp.int32, (rows, cols), 0) + feature0
    col = lax.broadcasted_iota(jnp.int32, (rows, cols), 1)
    inner = col & (ROWS - 1)
    hit = (feature == chunk * 208 + STRIP * (col >> 4) + inner) & (inner < STRIP)
    return jnp.where(hit, 1.0, 0.0).astype(BF16)


def dot(a, b, dims=((1,), (0,))):
    return lax.dot_general(a, b, (dims, ((), ())), preferred_element_type=F32)


HALVES = ((0, 896), (896, 768))


def attention_kernel(
    images, attn_gain, mlp_gain, strips, residual_out, routed_out,
    wg, expanded, acc, outp, summed, landed, stats, stats_in,
    s1_send, s1_recv, ring_send, ring_recv, core_send, core_recv, x_send, x_recv, t_send, t_recv, st_send, st_recv,
):
    x, y, z, c = place()

    def xdev(d):
        return device((x + d) % NX, y, z, c)

    def ydev(d):
        return device(x, (y + d) % NY, z, c)

    def zdev(d):
        return device(x, y, (z + d) % NZ, c)

    core = device(x, y, z, 1 - c)

    @pl.when(x != 0)
    def _():
        landed[:, :, QW:QP] = jnp.zeros((3, PATCHES, QP - QW), BF16)

    wg[z, y, c] = strips[...]
    greet([xdev(d) for d in (1, 2, 3)] + [ydev(d) for d in range(1, NY)] + [zdev(d) for d in range(1, NZ)] + [core])

    first = []
    for half, (lane, width) in enumerate(HALVES):
        for d in range(1, 8):
            target = zdev(d) if half == 0 else ydev(d)
            piece = wg.at[z, y, c, :, lane : lane + width]
            copy = remote(piece, piece, s1_send.at[half, d - 1], s1_recv.at[half, d - 1], target)
            copy.start()
            first.append(copy)

    values = images[...].astype(F32)
    center = values - jnp.mean(values, axis=-1, keepdims=True)
    spread = jnp.mean(center * center, axis=-1, keepdims=True)
    normed = (center * lax.rsqrt(spread + 1e-06) * attn_gain[...]).astype(BF16)
    for m in range(8):
        low = (208 * m) // 128 * 128
        wide = min(384, D - low)
        expanded[m] = dot(normed[:, low : low + wide], strip_pick(low, wide, m, 256)).astype(BF16)

    for copy in first:
        copy.wait()

    def block(half, pos, part):
        lane, width = HALVES[half]
        if half == 0:
            return wg.at[pl.ds(4 * part, 4), pos % NY, c, :, lane : lane + width]
        return wg.at[pos % NZ, pl.ds(4 * part, 4), c, :, lane : lane + width]

    def here(half):
        return y if half == 0 else z

    def ring_copy(half, way, step, part):
        pos = here(half) - (step - 1) if way == 0 else here(half) + (step - 1)
        piece = block(half, pos + 8, part)
        sign = 1 if way == 0 else -1
        target = ydev(8 + sign) if half == 0 else zdev(8 + sign)
        index = (step - 1) * 2 + part
        return remote(piece, piece, ring_send.at[half, way, index], ring_recv.at[half, way, index], target)

    def core_copy(half, slot, pos, part):
        piece = block(half, pos + 8, part)
        return remote(piece, piece, core_send.at[half, slot], core_recv.at[half, slot], core)

    started = []
    for part in range(2):
        for half in range(2):
            for way in range(2):
                copy = ring_copy(half, way, 1, part)
                copy.start()
                started.append(copy)
    for part in range(2):
        for half in range(2):
            copy = core_copy(half, part, here(half), part)
            copy.start()
            started.append(copy)
    slot = 2
    for step in range(1, 5):
        for part in range(2):
            for way in range(2):
                if step == 4 and part != way:
                    continue
                for half in range(2):
                    ring_copy(half, way, step, part).wait_recv()
                    if step < 3 or (step == 3 and part == way):
                        copy = ring_copy(half, way, step + 1, part)
                        copy.start()
                        started.append(copy)
                    pos = here(half) - step if way == 0 else here(half) + step
                    copy = core_copy(half, slot, pos, part)
                    copy.start()
                    started.append(copy)
                slot += 1
    for copy in started:
        copy.wait_send()
    for half in range(2):
        for index in range(16):
            core_copy(half, index, here(half), 0).wait_recv()

    def project(k, carry):
        weights = wg[k].reshape(256, D)
        part = dot(expanded[k], weights[:, 0:1280])

        @pl.when(k == 0)
        def _():
            acc[...] = part

        @pl.when(k > 0)
        def _():
            acc[...] += part

        return carry

    lax.fori_loop(0, 8, project, 0)
    lane = lax.broadcasted_iota(jnp.int32, (1, QP), 1)
    query = pltpu.roll(acc[:, 0:512].astype(BF16).astype(F32), 32, 1)
    keys = acc[:, 384:896].astype(BF16)
    vals = acc[:, 768:1280].astype(BF16).astype(F32)
    keys = jnp.where((lane >= 32) & (lane < 448), keys.astype(F32), 0.0).astype(BF16)
    mixed = jnp.zeros((PATCHES, QP), F32)
    for h in range(HEADS_HERE):
        in_q = (lane >= 32 + HEAD_DIM * h) & (lane < 32 + HEAD_DIM * (h + 1))
        in_v = (lane >= 64 + HEAD_DIM * h) & (lane < 64 + HEAD_DIM * (h + 1))
        scores = dot(jnp.where(in_q, query, 0.0).astype(BF16), keys, ((1,), (1,))) * HEAD_DIM ** (-0.5)
        top = jnp.max(scores, axis=-1, keepdims=True)
        grown = jnp.exp(scores - top)
        probs = (grown / jnp.sum(grown, axis=-1, keepdims=True)).astype(BF16)
        mixed += dot(probs, jnp.where(in_v, vals, 0.0).astype(BF16))
    heads = pltpu.roll(mixed.astype(BF16).astype(F32), 32, 1)
    heads = jnp.where(lane >= 96, heads, 0.0).astype(BF16)

    def spread_out(k, carry):
        weights = wg[k].reshape(256, D)
        outp[k] = dot(heads, weights[:, 1152:1664], ((1,), (1,))).astype(BF16)
        return carry

    lax.fori_loop(0, 8, spread_out, 0)
    for t in range(13):
        total = None
        for m in range(128 * t // 208, (128 * t + 127) // 208 + 1):
            term = dot(outp[m], strip_pick(128 * t, 128, m, 256), ((1,), (1,)))
            total = term if total is None else total + term
        summed[:, 128 * t : 128 * t + 128] = total.astype(BF16)

    def quarter(q):
        return pl.ds(pl.multiple_of(q * QW, 128), QW)

    def sum_copy(d):
        return remote(
            summed.at[:, quarter((x + d) % NX)], landed.at[d - 1, :, 0:QW], x_send.at[d - 1], x_recv.at[d - 1], xdev(d)
        )

    def tail_copy(d):
        return remote(
            summed.at[:, 4 * QW : D], landed.at[d - 1, :, QW:QP], t_send.at[d - 1], t_recv.at[d - 1], xdev(d)
        )

    for d in (2, 1, 3):
        sum_copy(d).start()

        @pl.when((x + d) % NX == 0)
        def _():
            tail_copy(d).start()

    has_tail = x == 0
    real = (lane < QW) | has_tail
    own = jnp.concatenate([summed[:, quarter(x)], summed[:, 4 * QW : D]], axis=1).astype(F32)
    base = jnp.concatenate([images[:, quarter(x)], images[:, 4 * QW : D]], axis=1).astype(F32)
    gain = jnp.concatenate([mlp_gain[:, quarter(x)], mlp_gain[:, 4 * QW : D]], axis=1)
    gain = jnp.where(real, gain, 0.0)
    for d in (1, 3, 2):
        sum_copy(d).wait()

        @pl.when((x + d) % NX == 0)
        def _():
            tail_copy(d).wait_send()

        @pl.when(has_tail)
        def _():
            tail_copy(d).wait_recv()

    attn = own + landed[0].astype(F32) + landed[1].astype(F32) + landed[2].astype(F32)
    residual = jnp.where(real, base + attn, 0.0)
    residual_out[...] = residual

    def width(q):
        return jnp.where(q == 0, 512.0, 384.0).astype(F32)

    mean_here = jnp.sum(residual, axis=-1, keepdims=True) / width(x)
    off = jnp.where(real, residual - mean_here, 0.0)
    dev_here = jnp.sum(off * off, axis=-1, keepdims=True)
    lane128 = lax.broadcasted_iota(jnp.int32, (1, 128), 1)
    packed = jnp.where(lane128 == 0, mean_here, jnp.where(lane128 == 1, dev_here, 0.0))
    stats[...] = packed.T[0:8, :]

    def stat_copy(d):
        return remote(stats, stats_in.at[d - 1], st_send.at[d - 1], st_recv.at[d - 1], xdev(d))

    for d in (1, 2, 3):
        stat_copy(d).start()
    for d in (1, 2, 3):
        stat_copy(d).wait()
    groups = [(stats[...], width(x))] + [(stats_in[d - 1], width((x + NX - d) % NX)) for d in (1, 2, 3)]
    mean = sum(g[0:1, :] * n for g, n in groups) / float(D)
    var = sum(g[1:2, :] + n * (g[0:1, :] - mean) * (g[0:1, :] - mean) for g, n in groups) / float(D)
    scale = lax.rsqrt(var + 1e-06)
    row = lax.broadcasted_iota(jnp.int32, (128, 256), 0)
    both = jnp.where(row == 0, mean, jnp.where(row == 1, scale, 0.0)).T
    routed_out[...] = ((residual - both[:, 0:1]) * both[:, 1:2] * gain).astype(BF16)


def attention(images, attn_gain, mlp_gain, strips):
    sem = pltpu.SemaphoreType.DMA
    vm = pl.BlockSpec(memory_space=pltpu.VMEM)
    return pl.pallas_call(
        attention_kernel,
        name="attention",
        out_shape=(jax.ShapeDtypeStruct((PATCHES, QP), F32), jax.ShapeDtypeStruct((PATCHES, QP), BF16)),
        in_specs=[vm] * 4,
        out_specs=(vm, vm),
        scratch_shapes=[
            pltpu.VMEM((NZ, NY, 2, ROWS, D), BF16),
            pltpu.VMEM((8, PATCHES, 256), BF16),
            pltpu.VMEM((PATCHES, 1280), F32),
            pltpu.VMEM((8, PATCHES, 256), BF16),
            pltpu.VMEM((PATCHES, D), BF16),
            pltpu.VMEM((3, PATCHES, QP), BF16),
            pltpu.VMEM((8, 256), F32),
            pltpu.VMEM((3, 8, 256), F32),
            sem((2, 7)), sem((2, 7)), sem((2, 2, 8)), sem((2, 2, 8)), sem((2, 16)), sem((2, 16)),
            sem((3,)), sem((3,)), sem((3,)), sem((3,)), sem((3,)), sem((3,)),
        ],
        compiler_params=pltpu.CompilerParams(collective_id=1, has_side_effects=True, vmem_limit_bytes=56 << 20),
    )(images, attn_gain.reshape(1, D), mlp_gain.reshape(1, D), strips)


def make_strips(qkv_weight, proj_weight):
    flat = jnp.concatenate([qkv_weight[0], qkv_weight[1], qkv_weight[2], proj_weight.T], axis=1)
    return jnp.pad(flat, ((0, ROWS - STRIP), (0, 0)))


def gelu_tanh(values):
    return 0.5 * values * (1.0 + jnp.tanh(0.7978845608028654 * (values + 0.044715 * values * values * values)))


def expert_kernel(
    routed, residual, slots, ids, gates, w_in_hbm, w_out_hbm, out,
    w_in, w_out, picked, by_z, by_pair, rows, parts, r1, q, r2a, r2b, sa, sb, r3a, r3b, res, back, by_image, home, final, gathered,
    w_sem, a_send, a_recv, b_send, b_recv, yp_send, yp_recv, xg_send, xg_recv, cg_send, cg_recv,
    r1_send, r1_recv, r2_send, r2_recv, r2y_send, r2y_recv, r3_send, r3_recv, r3y_send, r3y_recv,
    bb_send, bb_recv, aa_send, aa_recv, f_send, f_recv,
):
    x, y, z, c = place()
    par, pair = y % 2, y // 2
    tail = x == 0

    def xdev(d):
        return device((x + d) % NX, y, z, c)

    def ydev(d):
        return device(x, (y + d) % NY, z, c)

    def zdev(d):
        return device(x, y, (z + d) % NZ, c)

    core = device(x, y, z, 1 - c)
    mate = device(x, y + 1 - 2 * par, z, c)

    def quarter(k):
        return pl.ds(pl.multiple_of(k * QW, 128), QW)

    loads = [
        pltpu.make_async_copy(w_in_hbm, w_in, w_sem.at[0]),
        pltpu.make_async_copy(w_out_hbm, w_out, w_sem.at[1]),
    ]
    for load in loads:
        load.start()
    landing = (r2a, sa)
    greet([xdev(d) for d in (1, 2, 3)] + [ydev(d) for d in (2, 4, 6)] + [zdev(d) for d in range(1, NZ)] + [core, mate])

    token = lax.broadcasted_iota(jnp.int32, (PATCHES, 256), 0)
    holds = token == slots[0:1, :]
    picked[...] = dot(jnp.where(holds, 1.0, 0.0).astype(BF16), routed[...], ((0,), (0,))).astype(BF16)

    def a_copy(d):
        to = (z + d) % NZ
        return remote(
            picked.at[pl.ds(pl.multiple_of(to * 32, 32), 32)],
            by_z.at[pl.ds(pl.multiple_of(z * 32, 32), 32)],
            a_send.at[d - 1], a_recv.at[d - 1], zdev(d),
        )

    for d in (4, 3, 5, 2, 6, 1, 7):
        a_copy(d).start()
    own = pl.ds(pl.multiple_of(z * 32, 32), 32)
    by_z[own] = picked[own]

    slot_lane = lax.broadcasted_iota(jnp.int32, (1, 256), 1)
    slot_expert = slot_lane >> 3
    usable = (slot_lane & 7) < slots[1:2, :]
    gate = jnp.where(ids[:, 0:1] == slot_expert, gates[:, 0:1].astype(F32), 0.0)
    gate += jnp.where(ids[:, 1:2] == slot_expert, gates[:, 1:2].astype(F32), 0.0)
    placing = jnp.where(holds & usable, gate, 0.0).astype(BF16)
    r_out = lax.broadcasted_iota(jnp.int32, (256, 256), 0)
    r_in = lax.broadcasted_iota(jnp.int32, (256, 256), 1)
    order = ((r_out >> 6) == ((r_in >> 3) & 3)) & (((r_out >> 3) & 7) == (r_in >> 5)) & ((r_out & 7) == (r_in & 7))
    order = jnp.where(order, 1.0, 0.0).astype(BF16)
    for d in range(1, NZ):
        a_copy(d).wait()
    by_pair[...] = dot(order, by_z[...]).astype(BF16)

    class Both:
        def __init__(self, main, extra, is_tail):
            self.main, self.extra, self.is_tail = main, extra, is_tail

        def start(self):
            self.main.start()
            pl.when(self.is_tail)(self.extra.start)

        def wait_send(self):
            self.main.wait_send()
            pl.when(self.is_tail)(self.extra.wait_send)

        def wait_recv(self):
            self.main.wait_recv()
            pl.when(self.is_tail)(self.extra.wait_recv)

    def pieces(src_main, dst_main, src_extra, dst_extra, send, recv, target, is_tail):
        return Both(
            remote(src_main, dst_main, send.at[0], recv.at[0], target),
            remote(src_extra, dst_extra, send.at[1], recv.at[1], target),
            is_tail,
        )

    def b_copy(i):
        d = 2 * i
        to = ((y + d) % NY) // 2
        src = pl.ds(pl.multiple_of(to * 64, 64), 64)
        dst = pl.ds(pl.multiple_of(pair * 64, 64), 64)
        return pieces(
            by_pair.at[src, 0:QW], rows.at[par, c, dst, quarter(x)],
            by_pair.at[src, QW:QP], rows.at[par, c, dst, 4 * QW : D],
            b_send.at[i - 1], b_recv.at[i - 1], ydev(d), tail,
        )

    for i in (2, 1, 3):
        b_copy(i).start()
    own = pl.ds(pl.multiple_of(pair * 64, 64), 64)
    rows[par, c, own, quarter(x)] = by_pair[own, 0:QW]

    @pl.when(tail)
    def _():
        rows[par, c, own, 4 * QW : D] = by_pair[own, QW:QP]

    for i in (1, 2, 3):
        b_copy(i).wait_recv()

    def same(parity, core_index, q_index, send, recv, target, is_tail):
        main = rows.at[parity, core_index, :, quarter(q_index)]
        extra = rows.at[parity, core_index, :, 4 * QW : D]
        return pieces(main, main, extra, extra, send, recv, target, is_tail)

    mate_copy = same(par, c, x, yp_send, yp_recv, mate, tail)
    mate_copy.start()

    def x_copy(k, d):
        parity = par if k == 0 else 1 - par
        return same(parity, c, x, xg_send.at[k, d - 1], xg_recv.at[k, d - 1], xdev(d), tail)

    def x_arrived(k, d):
        from_tail = (x + NX - d) % NX == 0
        parity = par if k == 0 else 1 - par
        return same(parity, c, x, xg_send.at[k, d - 1], xg_recv.at[k, d - 1], xdev(d), from_tail)

    def core_copy(k, d):
        from_x = (x + NX - d) % NX
        parity = par if k == 0 else 1 - par
        return same(parity, c, from_x, cg_send.at[k, d], cg_recv.at[k, d], core, from_x == 0)

    for d in (2, 1, 3):
        x_copy(0, d).start()
    core_copy(0, 0).start()
    mate_copy.wait_recv()
    for d in (2, 1, 3):
        x_copy(1, d).start()
    core_copy(1, 0).start()
    for d in (1, 3, 2):
        x_arrived(0, d).wait_recv()
        core_copy(0, d).start()
    for load in loads:
        load.wait()

    def expert(parity, core_index):
        hidden = gelu_tanh(dot(rows[parity, core_index], w_in[...])).astype(BF16)
        parts[parity, core_index] = dot(hidden, w_out[...]).astype(BF16)

    def r1_copy(k):
        parity = par if k == 0 else 1 - par
        return remote(parts.at[parity, 1 - c], r1.at[parity], r1_send.at[k], r1_recv.at[k], core)

    for d in range(4):
        core_copy(0, d).wait_recv()
    expert(par, 1 - c)
    r1_copy(0).start()
    expert(par, c)
    for d in (1, 3, 2):
        x_arrived(1, d).wait_recv()
        core_copy(1, d).start()
    for d in range(4):
        core_copy(1, d).wait_recv()
    expert(1 - par, 1 - c)
    r1_copy(1).start()
    expert(1 - par, c)
    r1_copy(0).wait_recv()
    r1_copy(1).wait_recv()

    for parity in range(2):
        q[parity] = (parts[parity, c].astype(F32) + r1[parity].astype(F32)).astype(BF16)

    def r2_copy(d):
        to = (x + d) % NX
        return pieces(
            q.at[:, 0:128, quarter(to)], r2a.at[d - 1, :, :, 0:QW],
            q.at[:, 0:128, 4 * QW : D], r2a.at[d - 1, :, :, QW:QP],
            r2_send.at[d - 1], r2_recv.at[d - 1], xdev(d), to == 0,
        )

    def r2y_copy():
        return remote(q.at[1 - par, 128:256], r2b, r2y_send, r2y_recv, mate)

    def got(copy):
        copy.main.wait_recv()
        pl.when(tail)(copy.extra.wait_recv)

    r2y_copy().start()
    for d in (2, 1, 3):
        r2_copy(d).start()
    r2y_copy().wait_recv()
    sb[...] = (q[par, 128:256].astype(F32) + r2b[...].astype(F32)).astype(BF16)

    def r3_copy(d):
        to = (x + d) % NX
        return pieces(
            sb.at[:, quarter(to)], r3b.at[d - 1, :, 0:QW],
            sb.at[:, 4 * QW : D], r3b.at[d - 1, :, QW:QP],
            r3_send.at[d - 1], r3_recv.at[d - 1], xdev(d), to == 0,
        )

    for d in (2, 1, 3):
        r3_copy(d).start()
    lane = lax.broadcasted_iota(jnp.int32, (1, QP), 1)
    real = (lane < QW) | tail
    for d in (1, 3, 2):
        got(r2_copy(d))
    for parity in range(2):
        total = jnp.concatenate([q[parity, 0:128, quarter(x)], q[parity, 0:128, 4 * QW : D]], axis=1).astype(F32)
        for d in (1, 2, 3):
            total += r2a[d - 1, parity].astype(F32)
        sa[parity] = jnp.where(real, total, 0.0).astype(BF16)

    def r3y_copy():
        return remote(sa.at[1 - par], r3a, r3y_send, r3y_recv, mate)

    r3y_copy().start()
    for d in (1, 3, 2):
        got(r3_copy(d))
    total = jnp.concatenate([sb[:, quarter(x)], sb[:, 4 * QW : D]], axis=1).astype(F32)
    for d in (1, 2, 3):
        total += r3b[d - 1].astype(F32)
    res[128:256] = jnp.where(real, total, 0.0).astype(BF16)
    r3y_copy().wait_recv()
    res[0:128] = (sa[par].astype(F32) + r3a[...].astype(F32)).astype(BF16)

    def bb_copy(i):
        d = 2 * i
        to = ((y + d) % NY) // 2
        return remote(
            res.at[pl.ds(pl.multiple_of(to * 64, 64), 64)], back.at[pl.ds(pl.multiple_of(pair * 64, 64), 64)],
            bb_send.at[i - 1], bb_recv.at[i - 1], ydev(d),
        )

    for i in (2, 1, 3):
        bb_copy(i).start()
    back[own] = res[own]
    for i in (1, 2, 3):
        bb_copy(i).wait_recv()
    by_image[...] = dot(order, back[...], ((0,), (0,))).astype(BF16)

    def aa_copy(d):
        to = (z + d) % NZ
        return remote(
            by_image.at[pl.ds(pl.multiple_of(to * 32, 32), 32)], home.at[pl.ds(pl.multiple_of(z * 32, 32), 32)],
            aa_send.at[d - 1], aa_recv.at[d - 1], zdev(d),
        )

    for d in (4, 3, 5, 2, 6, 1, 7):
        aa_copy(d).start()
    own_z = pl.ds(pl.multiple_of(z * 32, 32), 32)
    home[own_z] = by_image[own_z]
    for d in range(1, NZ):
        aa_copy(d).wait_recv()
    final[...] = (residual[...] + dot(placing, home[...])).astype(BF16)

    def f_copy(d):
        to = pl.ds(pl.multiple_of((x + d) % NX * 64, 64), 64)
        return pieces(
            final.at[to, 0:QW], gathered.at[:, quarter(x)],
            final.at[to, QW:QP], gathered.at[:, 4 * QW : D],
            f_send.at[d - 1], f_recv.at[d - 1], xdev(d), tail,
        )

    for d in (2, 1, 3):
        f_copy(d).start()
    mine = pl.ds(pl.multiple_of(x * 64, 64), 64)
    gathered[:, quarter(x)] = final[mine, 0:QW]

    @pl.when(tail)
    def _():
        gathered[:, 4 * QW : D] = final[mine, QW:QP]

    for d in (1, 3, 2):
        copy = f_copy(d)
        copy.main.wait_recv()
        pl.when((x + NX - d) % NX == 0)(copy.extra.wait_recv)
    out[...] = gathered[...]

    for d in range(1, NZ):
        aa_copy(d).wait_send()
    for i in (1, 2, 3):
        b_copy(i).wait_send()
        bb_copy(i).wait_send()
    mate_copy.wait_send()
    for k in range(2):
        for d in (1, 2, 3):
            x_copy(k, d).wait_send()
        for d in range(4):
            core_copy(k, d).wait_send()
        r1_copy(k).wait_send()
    for d in (1, 2, 3):
        r2_copy(d).wait_send()
        r3_copy(d).wait_send()
        f_copy(d).wait_send()
    r2y_copy().wait_send()
    r3y_copy().wait_send()


def experts(routed, residual, slots, ids, gates, w_in, w_out):
    sem = pltpu.SemaphoreType.DMA
    vm = pl.BlockSpec(memory_space=pltpu.VMEM)
    hbm = pl.BlockSpec(memory_space=pl.ANY)
    v = lambda *s: pltpu.VMEM(s, BF16)
    return pl.pallas_call(
        expert_kernel,
        name="experts",
        out_shape=jax.ShapeDtypeStruct((64, D), BF16),
        in_specs=[vm] * 5 + [hbm] * 2,
        out_specs=vm,
        scratch_shapes=[
            v(D, 512), v(512, D), v(256, QP), v(256, QP), v(256, QP), v(2, 2, 256, D), v(2, 2, 256, D), v(2, 256, D),
            v(2, 256, D), v(3, 2, 128, QP), v(128, D), v(2, 128, QP), v(128, D), v(128, QP), v(3, 128, QP),
            v(256, QP), v(256, QP), v(256, QP), v(256, QP), v(256, QP), v(64, D),
            sem((2,)), sem((7,)), sem((7,)), sem((3, 2)), sem((3, 2)), sem((2,)), sem((2,)),
            sem((2, 3, 2)), sem((2, 3, 2)), sem((2, 4, 2)), sem((2, 4, 2)),
            sem((2,)), sem((2,)), sem((3, 2)), sem((3, 2)), sem, sem, sem((3, 2)), sem((3, 2)), sem, sem,
            sem((3,)), sem((3,)), sem((7,)), sem((7,)), sem((3, 2)), sem((3, 2)),
        ],
        compiler_params=pltpu.CompilerParams(collective_id=2, has_side_effects=True, vmem_limit_bytes=56 << 20),
    )(routed, residual, slots, ids, gates, w_in, w_out)


def on_device(
    images, attn_gain, qkv_weight, proj_weight, mlp_gain, expert_in, expert_out,
    gate_values, expert_ids, kept_patches, kept_counts,
):
    residual, routed = attention(images, attn_gain, mlp_gain, make_strips(qkv_weight, proj_weight))
    slots = jnp.concatenate(
        [kept_patches.reshape(1, 256), jnp.repeat(kept_counts.reshape(1, EXPERTS), 8, axis=1), jnp.zeros((6, 256), jnp.int32)], axis=0
    )
    return experts(routed, residual, slots, expert_ids, gate_values, expert_in, expert_out)


def solution(mesh):
    placed = (
        P("dp", None), P(), P(None, "dp", "mp"), P("mp", "dp"), P(), P(None, ("dp", "mp")), P(("dp", "mp"), None),
        P("dp", None), P("dp", None), P("dp", None, None), P("dp", None),
    )
    return jax.shard_map(on_device, mesh=mesh, in_specs=placed, out_specs=P(("dp", "mp"), None), check_vma=False)
```

time: 495 us -> 173 us (0.35)
  the two profiles are of different devices: /device:TPU:8 before, /device:TPU:2 now
where the time goes in v1:
time: 173 us; the launch traced here: 172 us
  Pallas kernels  161 us (93%)
  local copies, waits for them, and re-layouts  11.1 us (6%)
    pallas_call x1, Pallas kernels, experts(): pl.pallas_call(expert_kernel, name='experts', out_shape=jax.ShapeDtypeStr...  88.3 us
    pallas_call x1, Pallas kernels, attention(): pl.pallas_call(attention_kernel, name='attention', out_shape=(jax.ShapeDt...  72.4 us
    unnamed x4, local copies, waits for them, and re-layouts  5.29 us

profile of v1, /device:TPU:2, one launch (start us, length us, event | category | flops | bytes accessed | tf_op | source)
XLA Modules:
  0.0 172.4 jit_solution(12146837186567973187)
XLA Ops:
  0.0 0.1 pad.7.clone
  0.1 1.3 reshape.14.attn_gain
  1.4 1.3 reshape.15.mlp_gain
  2.7 0.8 copy.15
  3.4 0.1 reshape.16
  3.5 0.7 broadcast_in_dim.8
  4.2 0.1 broadcast_in_dim.9
  4.3 0.7 add_add_fusion.slots
  5.0 0.8 slice_bitcast_fusion
  5.8 0.8 concatenate.6
  6.6 0.6 pad.4.strips
  7.2 1.4 copy.17.gates
  8.6 1.5 copy.16.ids
  10.1 72.4 %attention.1 = (f32[256,512]{1,0:T(8,128)}, bf16[256,512]{1,0:T(8,128)(2,1)}) custom-call(bf16[256,1664]{1,0:T(8,128)(2,1)} %images.1, f32[1,1664]{1,0:T(1,128)} %reshape.14.attn_gain, f32[1,1664]{1,0:T(1,128)} %reshape.15.mlp_gain, bf16[16,1664]{1,0:T(8,128)(2,1)} %pad.4.strips), custom_call_target="tpu_custom_call" | custom-call | tf_op jit(solution)/shard_map/attention/pallas_call | solution.py:279
  82.5 88.3 %experts.1 = bf16[64,1664]{1,0:T(8,128)(2,1)} custom-call(bf16[256,512]{1,0:T(8,128)(2,1)} %get-tuple-element.7.routed, f32[256,512]{1,0:T(8,128)} %get-tuple-element.8.residual, s32[8,256]{1,0:T(8,128)} %add_add_fusion.slots, s32[256,2]{1,0:T(8,128)} %copy.16.ids, bf16[256,2]{1,0:T(8,128)(2,1)} %copy.17.gates, bf16[1664,512]{1,0:T(8,128)(2,1)} %w_in_hbm.1, ...), custom_call_target="tpu_custom_call" | custom-call | tf_op jit(solution)/shard_map/experts/pallas_call | solution.py:616
  170.8 1.6 copy.19
  (1 shorter events, 0.0 us)

commit v2 on v1

v2 whole, which is shorter than its diff:
```python
import functools

import jax
import jax.numpy as jnp
from jax import lax
from jax.experimental import pallas as pl
from jax.experimental.pallas import tpu as pltpu
from jax.sharding import PartitionSpec as P

MESH = pl.DeviceIdType.MESH
EXPERTS = 32
PATCHES = 256
HEAD_DIM = 104
HEADS_HERE = 4
D = 1664
NX, NY, NZ = 4, 8, 8
STRIP = 13
ROWS = 16
QW = 384
QP = 512
F32 = jnp.float32
BF16 = jnp.bfloat16


def place():
    dp = lax.axis_index("dp")
    return lax.axis_index("mp"), (dp // 2) % NY, dp // (2 * NY), dp % 2


def device(x, y, z, c):
    return ((z * NY + y) * 2 + c, x)


def remote(src, dst, send, recv, target):
    return pltpu.make_async_remote_copy(
        src_ref=src, dst_ref=dst, send_sem=send, recv_sem=recv, device_id=target, device_id_type=MESH
    )


def greet(partners):
    barrier = pltpu.get_barrier_semaphore()
    for partner in partners:
        pl.semaphore_signal(barrier, inc=1, device_id=partner, device_id_type=MESH)
    pl.semaphore_wait(barrier, len(partners))


def gelu_tanh(values):
    return 0.5 * values * (1.0 + jnp.tanh(0.7978845608028654 * (values + 0.044715 * values * values * values)))


def dot(a, b, dims=((1,), (0,))):
    return lax.dot_general(a, b, (dims, ((), ())), preferred_element_type=F32)


CUT = 896
OFFSETS = (0, 1, -1, 2, -2, 3, -3, 4)
CHUNKS = ((0, 1), (1, 3), (3, 5), (5, 8))


def slot_offset(s):
    return jnp.where(s % 2 == 1, (s + 1) // 2, -(s // 2))


def block_kernel(
    images, attn_gain, mlp_gain, qkv, proj, ids_t, gates_t, kept, counts, w_in_hbm, w_out_hbm, out,
    wg0, wg1, scratch_strip, exp0, exp1, acc, outp, summed, landed, stats, stats_in,
    w_in, w_out, picked, by_z, by_pair, rows, parts, r1, q, r2a, r2b, sa, sb, r3a, r3b, res, back, by_image, home, final, gathered,
    s1_send, s1_recv, ring_send, ring_recv, core_send, core_recv, x_send, x_recv, t_send, t_recv, st_send, st_recv,
    w_sem, a_send, a_recv, b_send, b_recv, yp_send, yp_recv, xg_send, xg_recv, cg_send, cg_recv,
    r1_send, r1_recv, r2_send, r2_recv, r2y_send, r2y_recv, r3_send, r3_recv, r3y_send, r3y_recv,
    bb_send, bb_recv, aa_send, aa_recv, f_send, f_recv,
):
    x, y, z, c = place()
    par, pair = y % 2, y // 2
    tail = x == 0

    def xdev(d):
        return device((x + d) % NX, y, z, c)

    def ydev(d):
        return device(x, (y + d) % NY, z, c)

    def zdev(d):
        return device(x, y, (z + d) % NZ, c)

    core = device(x, y, z, 1 - c)
    mate = device(x, y + 1 - 2 * par, z, c)

    def quarter(k):
        return pl.ds(pl.multiple_of(k * QW, 128), QW)

    near = [ydev(1), ydev(NY - 1), zdev(1), zdev(NZ - 1), core, xdev(1), xdev(3), xdev(2)]
    barrier = pltpu.get_barrier_semaphore()
    for partner in near:
        pl.semaphore_signal(barrier, inc=1, device_id=partner, device_id_type=MESH)
    loads = [
        pltpu.make_async_copy(w_in_hbm, w_in, w_sem.at[0]),
        pltpu.make_async_copy(w_out_hbm, w_out, w_sem.at[1]),
    ]
    for load in loads:
        load.start()

    scratch_strip[...] = jnp.zeros_like(scratch_strip)
    for i in range(3):
        scratch_strip[i, 0:STRIP, 0:416] = qkv[i].astype(F32)
    scratch_strip[3, 0:STRIP, 0:416] = proj[...].astype(F32)
    strip = scratch_strip[0]
    for i in range(1, 4):
        strip += pltpu.roll(scratch_strip[i], 416 * i, 1)
    strip = strip.astype(BF16)
    wg0[0, y, c] = strip[:, 0:CUT]
    wg1[z, 0, c] = strip[:, CUT:D]

    pl.semaphore_wait(barrier, len(near))

    def ring(half, stage, sign):
        along_z = (half == 0) == (stage == 1)
        return zdev(sign + NZ) if along_z else ydev(sign + NY)

    def first_copy(half, slot):
        source = 0 if slot < 3 else slot - 2
        if half == 0:
            src, dst = wg0.at[source, y, c], wg0.at[slot, y, c]
        else:
            src, dst = wg1.at[z, source, c], wg1.at[z, slot, c]
        return remote(
            src, dst, s1_send.at[half, slot - 1], s1_recv.at[half, slot - 1], ring(half, 1, -1 if slot % 2 else 1)
        )

    def chunk_ref(half, pos, k):
        low, high = CHUNKS[k]
        if half == 0:
            return wg0.at[low:high, pos % NY, c]
        return wg1.at[pos % NZ, low:high, c]

    def here(half):
        return y if half == 0 else z

    def ring_copy(half, way, step, k):
        pos = here(half) - (step - 1) if way == 0 else here(half) + (step - 1)
        piece = chunk_ref(half, pos + 8, k)
        index = (step - 1) * 4 + k
        return remote(
            piece, piece, ring_send.at[half, way, index], ring_recv.at[half, way, index], ring(half, 2, 1 if way == 0 else -1)
        )

    def core_copy_w(half, slot, pos, k):
        piece = chunk_ref(half, pos + 8, k)
        return remote(piece, piece, core_send.at[half, slot], core_recv.at[half, slot], core)

    started, core_list = [], []

    def go(copy):
        copy.start()
        started.append(copy)

    core_slots = [0, 0]

    def share(half, pos, k):
        copy = core_copy_w(half, core_slots[half], pos, k)
        core_slots[half] += 1
        go(copy)
        core_list.append(copy)

    def begin(k):
        for half in range(2):
            for way in range(2):
                go(ring_copy(half, way, 1, k))
        for half in range(2):
            share(half, here(half), k)

    def last_way(k):
        return 0 if k in (0, 3) else 1

    def advance(k, step):
        for way in range(2):
            if step == 4 and way != last_way(k):
                continue
            for half in range(2):
                ring_copy(half, way, step, k).wait_recv()
                if step < 3 or (step == 3 and way == last_way(k)):
                    go(ring_copy(half, way, step + 1, k))
                share(half, here(half) - step if way == 0 else here(half) + step, k)

    for half in range(2):
        go(first_copy(half, 1))
        go(first_copy(half, 2))
    begin(0)

    values = images[...].astype(F32)
    center = values - jnp.mean(values, axis=-1, keepdims=True)
    spread = jnp.mean(center * center, axis=-1, keepdims=True)
    normed = (center * lax.rsqrt(spread + 1e-06) * attn_gain[...].reshape(1, D)).astype(BF16)

    col = lax.broadcasted_iota(jnp.int32, (1, 256), 1)
    inner = col & (ROWS - 1)
    own_slot = col >> 5
    absolute = jnp.where(inner < STRIP, STRIP * (col >> 4) + inner, -4096)
    turned = ((y + NY + slot_offset(own_slot)) % NY) * 2 + ((col >> 4) & 1)
    relative = jnp.where(inner < STRIP, STRIP * turned + inner, -4096)

    def strip_pick(first, count, target):
        feature = lax.broadcasted_iota(jnp.int32, (count, 256), 0) + first
        return jnp.where(feature == target, 1.0, 0.0).astype(BF16)

    def expand(m):
        low = (208 * m) // 128 * 128
        wide = min(384, D - low)
        exp0[m] = dot(normed[:, low : low + wide], strip_pick(low - 208 * m, wide, absolute)).astype(BF16)
        exp1[m] = dot(normed[:, low : low + wide], strip_pick(low - 208 * m, wide, relative)).astype(BF16)

    for half in range(2):
        for slot in (1, 2):
            first_copy(half, slot).wait_recv()
            go(first_copy(half, slot + 2))
    begin(1)
    advance(0, 1)
    for half in range(2):
        for slot in (3, 4):
            first_copy(half, slot).wait_recv()
            go(first_copy(half, slot + 2))
    begin(2)
    advance(1, 1)
    advance(0, 2)
    expand(0)
    for half in range(2):
        for slot in (5, 6):
            first_copy(half, slot).wait_recv()
        go(first_copy(half, 7))
    advance(2, 1)
    advance(1, 2)
    expand(1)
    for half in range(2):
        first_copy(half, 7).wait_recv()
    begin(3)
    advance(0, 3)
    expand(2)
    for wave in range(4, 8):
        for k in (3, 2, 1, 0):
            step = wave - k
            if 1 <= step <= 4:
                advance(k, step)
        if wave < 7:
            expand(2 * wave - 5)
            if 2 * wave - 4 < 8:
                expand(2 * wave - 4)

    slot_col = lax.broadcasted_iota(jnp.int32, (256, 32), 0)
    expert_col = lax.broadcasted_iota(jnp.int32, (256, 32), 1)
    of_expert = jnp.where((slot_col >> 3) == expert_col, 1.0, 0.0)
    patch8 = dot(of_expert.astype(BF16), kept[...].astype(F32).astype(BF16), ((1,), (1,)))
    which = (lax.broadcasted_iota(jnp.int32, (256, 8), 0) & 7) == lax.broadcasted_iota(jnp.int32, (256, 8), 1)
    patch = jnp.sum(jnp.where(which, patch8, 0.0), axis=1, keepdims=True)
    valid = jnp.sum(of_expert * counts[...].astype(F32), axis=1, keepdims=True)
    lane128 = lax.broadcasted_iota(jnp.int32, (1, 128), 1)
    slot_rows = jnp.where(lane128 == 0, patch, jnp.where(lane128 == 1, valid, 0.0)).T
    row128 = lax.broadcasted_iota(jnp.int32, (128, 256), 0)
    meta = jnp.where(row128 == 0, ids_t[0:1, :].astype(F32), 0.0)
    meta = jnp.where(row128 == 1, ids_t[1:2, :].astype(F32), meta)
    meta = jnp.where(row128 == 2, gates_t[0:1, :].astype(F32), meta)
    meta = jnp.where(row128 == 3, gates_t[1:2, :].astype(F32), meta).T
    token = lax.broadcasted_iota(jnp.int32, (PATCHES, 256), 0)
    holds = token == slot_rows[0:1, :].astype(jnp.int32)
    slot_lane = lax.broadcasted_iota(jnp.int32, (1, 256), 1)
    slot_expert = (slot_lane >> 3).astype(F32)
    usable = (slot_lane & 7).astype(F32) < slot_rows[1:2, :]
    gate = jnp.where(meta[:, 0:1] == slot_expert, meta[:, 2:3], 0.0)
    gate += jnp.where(meta[:, 1:2] == slot_expert, meta[:, 3:4], 0.0)
    placing = jnp.where(holds & usable, gate, 0.0).astype(BF16)
    choosing = jnp.where(holds, 1.0, 0.0).astype(BF16)
    r_out = lax.broadcasted_iota(jnp.int32, (256, 256), 0)
    r_in = lax.broadcasted_iota(jnp.int32, (256, 256), 1)
    order = ((r_out >> 6) == ((r_in >> 3) & 3)) & (((r_out >> 3) & 7) == (r_in >> 5)) & ((r_out & 7) == (r_in & 7))
    order = jnp.where(order, 1.0, 0.0).astype(BF16)

    for copy in core_list:
        copy.wait_recv()

    acc[...] = jnp.zeros_like(acc)

    def project(k, carry):
        acc[:, 0:CUT] += dot(exp0[(z + NZ + slot_offset(k)) % NZ], wg0[k].reshape(256, CUT))
        acc[:, CUT:1280] += dot(exp1[k], wg1[k].reshape(256, D - CUT)[:, 0 : 1280 - CUT])
        return carry

    lax.fori_loop(0, 8, project, 0)
    lane = lax.broadcasted_iota(jnp.int32, (1, QP), 1)
    keys = acc[:, 384:896].astype(BF16).astype(F32)
    keys = jnp.where((lane >= 32) & (lane < 448), keys, 0.0).astype(BF16)
    vals = acc[:, 768:1280].astype(BF16).astype(F32)

    def sum_copy(h, d):
        return remote(
            summed.at[128 * h : 128 * h + 128, quarter((x + d) % NX)], landed.at[h, d - 1, :, 0:QW],
            x_send.at[h, d - 1], x_recv.at[h, d - 1], xdev(d),
        )

    def tail_copy(h, d):
        return remote(
            summed.at[128 * h : 128 * h + 128, 4 * QW : D], landed.at[h, d - 1, :, QW:QP],
            t_send.at[h, d - 1], t_recv.at[h, d - 1], xdev(d),
        )

    for half_rows in range(2):
        low = 128 * half_rows
        query = pltpu.roll(acc[low : low + 128, 0:512].astype(BF16).astype(F32), 32, 1)
        mixed = jnp.zeros((128, QP), F32)
        for h in range(HEADS_HERE):
            in_q = (lane >= 32 + HEAD_DIM * h) & (lane < 32 + HEAD_DIM * (h + 1))
            in_v = (lane >= 64 + HEAD_DIM * h) & (lane < 64 + HEAD_DIM * (h + 1))
            scores = dot(jnp.where(in_q, query, 0.0).astype(BF16), keys, ((1,), (1,))) * HEAD_DIM ** (-0.5)
            top = jnp.max(scores, axis=-1, keepdims=True)
            grown = jnp.exp(scores - top)
            probs = (grown / jnp.sum(grown, axis=-1, keepdims=True)).astype(BF16)
            mixed += dot(probs, jnp.where(in_v, vals, 0.0).astype(BF16))
        heads = pltpu.roll(mixed.astype(BF16).astype(F32), 32, 1)
        heads = jnp.where(lane >= 96, heads, 0.0).astype(BF16)

        def spread_out(k, carry, low=low, heads=heads):
            weights = wg1[k].reshape(256, D - CUT)[:, 1152 - CUT : D - CUT]
            outp[k, low : low + 128, :] = dot(heads, weights, ((1,), (1,))).astype(BF16)
            return carry

        lax.fori_loop(0, 8, spread_out, 0)
        for t in range(13):
            total = None
            for m in range(128 * t // 208, (128 * t + 127) // 208 + 1):
                term = dot(outp[m, low : low + 128, :], strip_pick(128 * t - 208 * m, 128, relative), ((1,), (1,)))
                total = term if total is None else total + term
            summed[low : low + 128, 128 * t : 128 * t + 128] = total.astype(BF16)
        for d in (2, 1, 3):
            go(sum_copy(half_rows, d))
            pl.when((x + d) % NX == 0)(tail_copy(half_rows, d).start)

    real = (lane < QW) | tail
    own = jnp.concatenate([summed[:, quarter(x)], summed[:, 4 * QW : D]], axis=1).astype(F32)
    base = jnp.concatenate([images[:, quarter(x)], images[:, 4 * QW : D]], axis=1).astype(F32)
    gain = jnp.concatenate([mlp_gain[quarter(x)], mlp_gain[4 * QW : D]]).reshape(1, QP)
    gain = jnp.where(real, gain, 0.0)
    for h in range(2):
        for d in (1, 3, 2):
            sum_copy(h, d).wait_recv()
            pl.when(tail)(tail_copy(h, d).wait_recv)

    attn = own
    for d in (1, 2, 3):
        attn += jnp.concatenate([landed[0, d - 1], landed[1, d - 1]], axis=0).astype(F32)
    residual = jnp.where(real, base + attn, 0.0)

    def width(k):
        return jnp.where(k == 0, 512.0, 384.0).astype(F32)

    mean_here = jnp.sum(residual, axis=-1, keepdims=True) / width(x)
    off = jnp.where(real, residual - mean_here, 0.0)
    dev_here = jnp.sum(off * off, axis=-1, keepdims=True)
    stats[...] = jnp.where(lane128 == 0, mean_here, jnp.where(lane128 == 1, dev_here, 0.0)).T[0:8, :]

    def stat_copy(d):
        return remote(stats, stats_in.at[d - 1], st_send.at[d - 1], st_recv.at[d - 1], xdev(d))

    for d in (2, 1, 3):
        go(stat_copy(d))
    for d in (1, 3, 2):
        stat_copy(d).wait_recv()
    groups = [(stats[...], width(x))] + [(stats_in[d - 1], width((x + NX - d) % NX)) for d in (1, 2, 3)]
    mean = sum(g[0:1, :] * n for g, n in groups) / float(D)
    var = sum(g[1:2, :] + n * (g[0:1, :] - mean) * (g[0:1, :] - mean) for g, n in groups) / float(D)
    scale = lax.rsqrt(var + 1e-06)
    both = jnp.where(row128 == 0, mean, jnp.where(row128 == 1, scale, 0.0)).T
    routed = ((residual - both[:, 0:1]) * both[:, 1:2] * gain).astype(BF16)
    picked[...] = dot(choosing, routed, ((0,), (0,))).astype(BF16)

    def a_copy(d):
        to = (z + d) % NZ
        return remote(
            picked.at[pl.ds(pl.multiple_of(to * 32, 32), 32)],
            by_z.at[pl.ds(pl.multiple_of(z * 32, 32), 32)],
            a_send.at[d - 1], a_recv.at[d - 1], zdev(d),
        )

    for d in (4, 3, 5, 2, 6, 1, 7):
        a_copy(d).start()
    own = pl.ds(pl.multiple_of(z * 32, 32), 32)
    by_z[own] = picked[own]

    for d in range(1, NZ):
        a_copy(d).wait()
    by_pair[...] = dot(order, by_z[...]).astype(BF16)

    class Both:
        def __init__(self, main, extra, is_tail):
            self.main, self.extra, self.is_tail = main, extra, is_tail

        def start(self):
            self.main.start()
            pl.when(self.is_tail)(self.extra.start)

        def wait_send(self):
            self.main.wait_send()
            pl.when(self.is_tail)(self.extra.wait_send)

        def wait_recv(self):
            self.main.wait_recv()
            pl.when(self.is_tail)(self.extra.wait_recv)

    def pieces(src_main, dst_main, src_extra, dst_extra, send, recv, target, is_tail):
        return Both(
            remote(src_main, dst_main, send.at[0], recv.at[0], target),
            remote(src_extra, dst_extra, send.at[1], recv.at[1], target),
            is_tail,
        )

    def b_copy(i):
        d = 2 * i
        to = ((y + d) % NY) // 2
        src = pl.ds(pl.multiple_of(to * 64, 64), 64)
        dst = pl.ds(pl.multiple_of(pair * 64, 64), 64)
        return pieces(
            by_pair.at[src, 0:QW], rows.at[par, c, dst, quarter(x)],
            by_pair.at[src, QW:QP], rows.at[par, c, dst, 4 * QW : D],
            b_send.at[i - 1], b_recv.at[i - 1], ydev(d), tail,
        )

    for i in (2, 1, 3):
        b_copy(i).start()
    own = pl.ds(pl.multiple_of(pair * 64, 64), 64)
    rows[par, c, own, quarter(x)] = by_pair[own, 0:QW]

    @pl.when(tail)
    def _():
        rows[par, c, own, 4 * QW : D] = by_pair[own, QW:QP]

    for i in (1, 2, 3):
        b_copy(i).wait_recv()

    def same(parity, core_index, q_index, send, recv, target, is_tail):
        main = rows.at[parity, core_index, :, quarter(q_index)]
        extra = rows.at[parity, core_index, :, 4 * QW : D]
        return pieces(main, main, extra, extra, send, recv, target, is_tail)

    mate_copy = same(par, c, x, yp_send, yp_recv, mate, tail)
    mate_copy.start()

    def x_copy(k, d):
        parity = par if k == 0 else 1 - par
        return same(parity, c, x, xg_send.at[k, d - 1], xg_recv.at[k, d - 1], xdev(d), tail)

    def x_arrived(k, d):
        from_tail = (x + NX - d) % NX == 0
        parity = par if k == 0 else 1 - par
        return same(parity, c, x, xg_send.at[k, d - 1], xg_recv.at[k, d - 1], xdev(d), from_tail)

    def core_copy(k, d):
        from_x = (x + NX - d) % NX
        parity = par if k == 0 else 1 - par
        return same(parity, c, from_x, cg_send.at[k, d], cg_recv.at[k, d], core, from_x == 0)

    for d in (2, 1, 3):
        x_copy(0, d).start()
    core_copy(0, 0).start()
    mate_copy.wait_recv()
    for d in (2, 1, 3):
        x_copy(1, d).start()
    core_copy(1, 0).start()
    for d in (1, 3, 2):
        x_arrived(0, d).wait_recv()
        core_copy(0, d).start()
    for load in loads:
        load.wait()

    def expert(parity, core_index):
        hidden = gelu_tanh(dot(rows[parity, core_index], w_in[...])).astype(BF16)
        parts[parity, core_index] = dot(hidden, w_out[...]).astype(BF16)

    def r1_copy(k):
        parity = par if k == 0 else 1 - par
        return remote(parts.at[parity, 1 - c], r1.at[parity], r1_send.at[k], r1_recv.at[k], core)

    for d in range(4):
        core_copy(0, d).wait_recv()
    expert(par, 1 - c)
    r1_copy(0).start()
    expert(par, c)
    for d in (1, 3, 2):
        x_arrived(1, d).wait_recv()
        core_copy(1, d).start()
    for d in range(4):
        core_copy(1, d).wait_recv()
    expert(1 - par, 1 - c)
    r1_copy(1).start()
    expert(1 - par, c)
    r1_copy(0).wait_recv()
    r1_copy(1).wait_recv()

    for parity in range(2):
        q[parity] = (parts[parity, c].astype(F32) + r1[parity].astype(F32)).astype(BF16)

    def r2_copy(d):
        to = (x + d) % NX
        return pieces(
            q.at[:, 0:128, quarter(to)], r2a.at[d - 1, :, :, 0:QW],
            q.at[:, 0:128, 4 * QW : D], r2a.at[d - 1, :, :, QW:QP],
            r2_send.at[d - 1], r2_recv.at[d - 1], xdev(d), to == 0,
        )

    def r2y_copy():
        return remote(q.at[1 - par, 128:256], r2b, r2y_send, r2y_recv, mate)

    def got(copy):
        copy.main.wait_recv()
        pl.when(tail)(copy.extra.wait_recv)

    r2y_copy().start()
    for d in (2, 1, 3):
        r2_copy(d).start()
    r2y_copy().wait_recv()
    sb[...] = (q[par, 128:256].astype(F32) + r2b[...].astype(F32)).astype(BF16)

    def r3_copy(d):
        to = (x + d) % NX
        return pieces(
            sb.at[:, quarter(to)], r3b.at[d - 1, :, 0:QW],
            sb.at[:, 4 * QW : D], r3b.at[d - 1, :, QW:QP],
            r3_send.at[d - 1], r3_recv.at[d - 1], xdev(d), to == 0,
        )

    for d in (2, 1, 3):
        r3_copy(d).start()
    for d in (1, 3, 2):
        got(r2_copy(d))
    for parity in range(2):
        total = jnp.concatenate([q[parity, 0:128, quarter(x)], q[parity, 0:128, 4 * QW : D]], axis=1).astype(F32)
        for d in (1, 2, 3):
            total += r2a[d - 1, parity].astype(F32)
        sa[parity] = jnp.where(real, total, 0.0).astype(BF16)

    def r3y_copy():
        return remote(sa.at[1 - par], r3a, r3y_send, r3y_recv, mate)

    r3y_copy().start()
    for d in (1, 3, 2):
        got(r3_copy(d))
    total = jnp.concatenate([sb[:, quarter(x)], sb[:, 4 * QW : D]], axis=1).astype(F32)
    for d in (1, 2, 3):
        total += r3b[d - 1].astype(F32)
    res[128:256] = jnp.where(real, total, 0.0).astype(BF16)
    r3y_copy().wait_recv()
    res[0:128] = (sa[par].astype(F32) + r3a[...].astype(F32)).astype(BF16)

    def bb_copy(i):
        d = 2 * i
        to = ((y + d) % NY) // 2
        return remote(
            res.at[pl.ds(pl.multiple_of(to * 64, 64), 64)], back.at[pl.ds(pl.multiple_of(pair * 64, 64), 64)],
            bb_send.at[i - 1], bb_recv.at[i - 1], ydev(d),
        )

    for i in (2, 1, 3):
        bb_copy(i).start()
    back[own] = res[own]
    for i in (1, 2, 3):
        bb_copy(i).wait_recv()
    by_image[...] = dot(order, back[...], ((0,), (0,))).astype(BF16)

    def aa_copy(d):
        to = (z + d) % NZ
        return remote(
            by_image.at[pl.ds(pl.multiple_of(to * 32, 32), 32)], home.at[pl.ds(pl.multiple_of(z * 32, 32), 32)],
            aa_send.at[d - 1], aa_recv.at[d - 1], zdev(d),
        )

    for d in (4, 3, 5, 2, 6, 1, 7):
        aa_copy(d).start()
    own_z = pl.ds(pl.multiple_of(z * 32, 32), 32)
    home[own_z] = by_image[own_z]
    for d in range(1, NZ):
        aa_copy(d).wait_recv()
    final[...] = (residual + dot(placing, home[...])).astype(BF16)

    def f_copy(d):
        to = pl.ds(pl.multiple_of((x + d) % NX * 64, 64), 64)
        return pieces(
            final.at[to, 0:QW], gathered.at[:, quarter(x)],
            final.at[to, QW:QP], gathered.at[:, 4 * QW : D],
            f_send.at[d - 1], f_recv.at[d - 1], xdev(d), tail,
        )

    for d in (2, 1, 3):
        f_copy(d).start()
    mine = pl.ds(pl.multiple_of(x * 64, 64), 64)
    gathered[:, quarter(x)] = final[mine, 0:QW]

    @pl.when(tail)
    def _():
        gathered[:, 4 * QW : D] = final[mine, QW:QP]

    for d in (1, 3, 2):
        copy = f_copy(d)
        copy.main.wait_recv()
        pl.when((x + NX - d) % NX == 0)(copy.extra.wait_recv)
    out[...] = gathered[...]

    for copy in started:
        copy.wait_send()
    for h in range(2):
        for d in (1, 2, 3):
            pl.when((x + d) % NX == 0)(tail_copy(h, d).wait_send)
    for d in range(1, NZ):
        aa_copy(d).wait_send()
    for i in (1, 2, 3):
        b_copy(i).wait_send()
        bb_copy(i).wait_send()
    mate_copy.wait_send()
    for k in range(2):
        for d in (1, 2, 3):
            x_copy(k, d).wait_send()
        for d in range(4):
            core_copy(k, d).wait_send()
        r1_copy(k).wait_send()
    for d in (1, 2, 3):
        r2_copy(d).wait_send()
        r3_copy(d).wait_send()
        f_copy(d).wait_send()
    r2y_copy().wait_send()
    r3y_copy().wait_send()


def block(images, attn_gain, mlp_gain, qkv, proj_t, ids_t, gates_t, kept, counts, w_in, w_out):
    sem = pltpu.SemaphoreType.DMA
    vm = pl.BlockSpec(memory_space=pltpu.VMEM)
    hbm = pl.BlockSpec(memory_space=pl.ANY)

    def v(*shape, kind=BF16):
        return pltpu.VMEM(shape, kind)

    return pl.pallas_call(
        block_kernel,
        name="block",
        out_shape=jax.ShapeDtypeStruct((64, D), BF16),
        in_specs=[vm] * 9 + [hbm] * 2,
        out_specs=vm,
        scratch_shapes=[
            v(8, NY, 2, ROWS, CUT), v(NZ, 8, 2, ROWS, D - CUT), v(4, ROWS, D, kind=F32),
            v(8, PATCHES, 256), v(8, PATCHES, 256), v(PATCHES, 1280, kind=F32), v(8, PATCHES, 256), v(PATCHES, D),
            v(2, 3, 128, QP), v(8, 256, kind=F32), v(3, 8, 256, kind=F32),
            v(D, 512), v(512, D), v(256, QP), v(256, QP), v(256, QP), v(2, 2, 256, D), v(2, 2, 256, D), v(2, 256, D),
            v(2, 256, D), v(3, 2, 128, QP), v(128, D), v(2, 128, QP), v(128, D), v(128, QP), v(3, 128, QP),
            v(256, QP), v(256, QP), v(256, QP), v(256, QP), v(256, QP), v(64, D),
            sem((2, 7)), sem((2, 7)), sem((2, 2, 16)), sem((2, 2, 16)), sem((2, 32)), sem((2, 32)),
            sem((2, 3)), sem((2, 3)), sem((2, 3)), sem((2, 3)), sem((3,)), sem((3,)),
            sem((2,)), sem((7,)), sem((7,)), sem((3, 2)), sem((3, 2)), sem((2,)), sem((2,)),
            sem((2, 3, 2)), sem((2, 3, 2)), sem((2, 4, 2)), sem((2, 4, 2)),
            sem((2,)), sem((2,)), sem((3, 2)), sem((3, 2)), sem, sem, sem((3, 2)), sem((3, 2)), sem, sem,
            sem((3,)), sem((3,)), sem((7,)), sem((7,)), sem((3, 2)), sem((3, 2)),
        ],
        compiler_params=pltpu.CompilerParams(collective_id=1, has_side_effects=True, vmem_limit_bytes=56 << 20),
    )(images, attn_gain, mlp_gain, qkv, proj_t, ids_t, gates_t, kept, counts, w_in, w_out)


def on_device(
    images, attn_gain, qkv_weight, proj_weight, mlp_gain, expert_in, expert_out,
    gate_values, expert_ids, kept_patches, kept_counts,
):
    return block(
        images, attn_gain, mlp_gain, qkv_weight, proj_weight.T, expert_ids.T, gate_values.T,
        kept_patches[0].T, kept_counts, expert_in, expert_out,
    )


def solution(mesh):
    placed = (
        P("dp", None), P(), P(None, "dp", "mp"), P("mp", "dp"), P(), P(None, ("dp", "mp")), P(("dp", "mp"), None),
        P("dp", None), P("dp", None), P("dp", None, None), P("dp", None),
    )
    return jax.shard_map(on_device, mesh=mesh, in_specs=placed, out_specs=P(("dp", "mp"), None), check_vma=False)
```

time: 173 us -> 156 us (0.902)
  the two profiles are of different devices: /device:TPU:2 before, /device:TPU:10 now
where the time goes in v2:
time: 156 us
  Pallas kernels  154 us (99%)
  local copies, waits for them, and re-layouts  1.63 us (1%)
    pallas_call x1, Pallas kernels, block(): pl.pallas_call(block_kernel, name='block', out_shape=jax.ShapeDtypeStruct...  154 us

profile of v2, /device:TPU:10, one launch (start us, length us, event | category | flops | bytes accessed | tf_op | source)
XLA Modules:
  0.0 155.6 jit_solution(3881548592378333272)
XLA Ops:
  0.0 153.9 %block.1 = bf16[64,1664]{1,0:T(8,128)(2,1)} custom-call(bf16[256,1664]{1,0:T(8,128)(2,1)} %images.1, f32[1664]{0:T(1024)} %attn_gain.1, f32[1664]{0:T(1024)} %mlp_gain.1, bf16[3,13,416]{2,1,0:T(8,128)(2,1)} %qkv.1, bf16[13,416]{1,0:T(8,128)(2,1)} %bitcast.6, s32[2,256]{1,0:T(2,128)} %bitcast.8, bf16[2,256]{1,0:T(2,128)(2,1)} %bitcast.9, s32[8,32]{1,0:T(8,128)} %bitcast.7, ...), custom_call_target="tpu_custom_call" | custom-call | tf_op jit(solution)/shard_map/block/pallas_call | solution.py:636
  153.9 1.6 %copy.13 = bf16[64,1664]{1,0:T(8,128)(2,1)} copy(bf16[64,1664]{1,0:T(8,128)(2,1)} %block.1) | data formatting | bytes 425984

commit v3 on v2

v3 whole, which is shorter than its diff:
```python
import functools

import jax
import jax.numpy as jnp
from jax import lax
from jax.experimental import pallas as pl
from jax.experimental.pallas import tpu as pltpu
from jax.sharding import PartitionSpec as P

MESH = pl.DeviceIdType.MESH
EXPERTS = 32
PATCHES = 256
HEAD_DIM = 104
HEADS_HERE = 4
D = 1664
NX, NY, NZ = 4, 8, 8
STRIP = 13
ROWS = 16
QW = 384
QP = 512
F32 = jnp.float32
BF16 = jnp.bfloat16


def place():
    dp = lax.axis_index("dp")
    return lax.axis_index("mp"), (dp // 2) % NY, dp // (2 * NY), dp % 2


def device(x, y, z, c):
    return ((z * NY + y) * 2 + c, x)


def remote(src, dst, send, recv, target):
    return pltpu.make_async_remote_copy(
        src_ref=src, dst_ref=dst, send_sem=send, recv_sem=recv, device_id=target, device_id_type=MESH
    )


def greet(partners):
    barrier = pltpu.get_barrier_semaphore()
    for partner in partners:
        pl.semaphore_signal(barrier, inc=1, device_id=partner, device_id_type=MESH)
    pl.semaphore_wait(barrier, len(partners))


def gelu_tanh(values):
    return 0.5 * values * (1.0 + jnp.tanh(0.7978845608028654 * (values + 0.044715 * values * values * values)))


def dot(a, b, dims=((1,), (0,))):
    return lax.dot_general(a, b, (dims, ((), ())), preferred_element_type=F32)


FAR = sorted(((i, d) for i in range(4) for d in range(8) if (i, d) != (0, 0)), key=lambda s: -(min(2 * s[0], 8 - 2 * s[0]) + min(s[1], 8 - s[1])))
FIRST = 176
CUT = 896
OFFSETS = (0, 1, -1, 2, -2, 3, -3, 4)
CHUNKS = ((0, 1), (1, 3), (3, 5), (5, 7), (7, 8))
ROUTE = (
    ("start", 0), ("first", 1), ("first", 2), ("start", 1), (1, 1, 0), (0, 1, 0), ("first", 3), ("first", 4), ("start", 2),
    (1, 1, 1), (0, 1, 1), (1, 2, 0), (0, 2, 0), ("first", 5), ("first", 6), ("start", 3), (1, 1, 2), (0, 1, 2), (1, 2, 1),
    (0, 2, 1), (1, 3, 0), (0, 3, 0), ("first", 7), ("start", 4), (0, 1, 3), (1, 1, 3), (0, 2, 2), (1, 2, 2), (0, 3, 1),
    (1, 3, 1), (0, 1, 4), (1, 4, 0), (1, 1, 4), (0, 2, 3), (1, 2, 3), (0, 3, 2), (0, 2, 4), (1, 3, 2), (0, 3, 3), (1, 4, 1),
    (1, 2, 4), (0, 3, 4), (1, 3, 3), (1, 4, 2), (0, 4, 3), (1, 3, 4), (0, 4, 4),
)


def slot_offset(s):
    return jnp.where(s % 2 == 1, (s + 1) // 2, -(s // 2))


def block_kernel(
    images_hbm, attn_gain_hbm, mlp_gain_hbm, qkv_hbm, proj_hbm, ids_hbm, gates_hbm, kept_hbm, counts_hbm,
    w_in_hbm, w_out_hbm, out,
    images, attn_gain, mlp_gain, qkv, proj, ids_t, gates_t, kept, counts,
    wg0, wg1, scratch_strip, exp0, exp1, acc, outp, summed, landed, stats, stats_in,
    w_in, w_out, picked, arrived, rows, parts, r1, q, r2a, r2c, r2b, sa, sb, r3a, r3b, returning, home, final, gathered,
    s1_send, s1_recv, ring_send, ring_recv, core_send, core_recv, x_send, x_recv, t_send, t_recv, st_send, st_recv,
    w_sem, a_send, a_recv, yp_send, yp_recv, xg_send, xg_recv, cg_send, cg_recv,
    r1_send, r1_recv, r2_send, r2_recv, r2c_send, r2c_recv, r2y_send, r2y_recv, r3_send, r3_recv, r3y_send, r3y_recv,
    aa_send, aa_recv, f_send, f_recv,
):
    x, y, z, c = place()
    par, pair = y % 2, y // 2
    tail = x == 0

    def xdev(d):
        return device((x + d) % NX, y, z, c)

    def ydev(d):
        return device(x, (y + d) % NY, z, c)

    def zdev(d):
        return device(x, y, (z + d) % NZ, c)

    core = device(x, y, z, 1 - c)
    mate = device(x, y + 1 - 2 * par, z, c)

    def quarter(k):
        return pl.ds(pl.multiple_of(k * QW, 128), QW)

    near = [ydev(1), ydev(NY - 1), zdev(1), zdev(NZ - 1), core, xdev(1), xdev(3), xdev(2)]
    barrier = pltpu.get_barrier_semaphore()
    for partner in near:
        pl.semaphore_signal(barrier, inc=1, device_id=partner, device_id_type=MESH)
    arguments = (
        (qkv_hbm, qkv), (proj_hbm, proj), (kept_hbm, kept), (counts_hbm, counts), (ids_hbm, ids_t), (gates_hbm, gates_t),
        (images_hbm, images), (attn_gain_hbm, attn_gain), (mlp_gain_hbm, mlp_gain), (w_in_hbm, w_in), (w_out_hbm, w_out),
    )
    loads = [pltpu.make_async_copy(src, dst, w_sem.at[i]) for i, (src, dst) in enumerate(arguments)]
    for load in loads:
        load.start()
    for load in loads[0:6]:
        load.wait()

    scratch_strip[...] = jnp.zeros_like(scratch_strip)
    for i in range(3):
        scratch_strip[i, 0:STRIP, 0:416] = qkv[i].astype(F32)
    scratch_strip[3, 0:STRIP, 0:416] = proj[...].astype(F32)
    strip = scratch_strip[0]
    for i in range(1, 4):
        strip += pltpu.roll(scratch_strip[i], 416 * i, 1)
    strip = strip.astype(BF16)
    wg0[0, y, c] = strip[:, 0:CUT]
    wg1[z, 0, c] = strip[:, CUT:D]

    slot_col = lax.broadcasted_iota(jnp.int32, (256, 32), 0)
    expert_col = lax.broadcasted_iota(jnp.int32, (256, 32), 1)
    of_expert = jnp.where((slot_col >> 3) == expert_col, 1.0, 0.0)
    patch8 = dot(of_expert.astype(BF16), kept[...].astype(F32).astype(BF16), ((1,), (1,)))
    which = (lax.broadcasted_iota(jnp.int32, (256, 8), 0) & 7) == lax.broadcasted_iota(jnp.int32, (256, 8), 1)
    patch = jnp.sum(jnp.where(which, patch8, 0.0), axis=1, keepdims=True)
    valid = jnp.sum(of_expert * counts[...].astype(F32), axis=1, keepdims=True)
    lane128 = lax.broadcasted_iota(jnp.int32, (1, 128), 1)
    slot_rows = jnp.where(lane128 == 0, patch, jnp.where(lane128 == 1, valid, 0.0)).T
    row128 = lax.broadcasted_iota(jnp.int32, (128, 256), 0)
    meta = jnp.where(row128 == 0, ids_t[0:1, :].astype(F32), 0.0)
    meta = jnp.where(row128 == 1, ids_t[1:2, :].astype(F32), meta)
    meta = jnp.where(row128 == 2, gates_t[0:1, :].astype(F32), meta)
    meta = jnp.where(row128 == 3, gates_t[1:2, :].astype(F32), meta).T
    token = lax.broadcasted_iota(jnp.int32, (PATCHES, 256), 0)
    holds = token == slot_rows[0:1, :].astype(jnp.int32)
    slot_lane = lax.broadcasted_iota(jnp.int32, (1, 256), 1)
    slot_expert = (slot_lane >> 3).astype(F32)
    usable = (slot_lane & 7).astype(F32) < slot_rows[1:2, :]
    gate = jnp.where(meta[:, 0:1] == slot_expert, meta[:, 2:3], 0.0)
    gate += jnp.where(meta[:, 1:2] == slot_expert, meta[:, 3:4], 0.0)
    placing = jnp.where(holds & usable, gate, 0.0).astype(BF16)
    choosing = jnp.where(holds, 1.0, 0.0).astype(BF16)

    acc[...] = jnp.zeros_like(acc)
    pl.semaphore_wait(barrier, len(near))

    def ring(half, stage, sign):
        along_z = (half == 0) == (stage == 1)
        return zdev(sign + NZ) if along_z else ydev(sign + NY)

    def first_copy(half, slot):
        source = 0 if slot < 3 else slot - 2
        if half == 0:
            src, dst = wg0.at[source, y, c], wg0.at[slot, y, c]
        else:
            src, dst = wg1.at[z, source, c], wg1.at[z, slot, c]
        return remote(
            src, dst, s1_send.at[half, slot - 1], s1_recv.at[half, slot - 1], ring(half, 1, -1 if slot % 2 else 1)
        )

    def chunk_ref(half, pos, k):
        low, high = CHUNKS[k]
        if half == 0:
            return wg0.at[low:high, pos % NY, c]
        return wg1.at[pos % NZ, low:high, c]

    def here(half):
        return y if half == 0 else z

    def ring_copy(half, way, step, k):
        pos = here(half) - (step - 1) if way == 0 else here(half) + (step - 1)
        piece = chunk_ref(half, pos + 8, k)
        index = (step - 1) * 5 + k
        return remote(
            piece, piece, ring_send.at[half, way, index], ring_recv.at[half, way, index], ring(half, 2, 1 if way == 0 else -1)
        )

    def core_copy_w(half, slot, pos, k):
        piece = chunk_ref(half, pos + 8, k)
        return remote(piece, piece, core_send.at[half, slot], core_recv.at[half, slot], core)

    started, core_list = [], [[] for _ in CHUNKS]

    def go(copy):
        copy.start()
        started.append(copy)

    core_slots = [0, 0]

    def share(half, pos, k):
        copy = core_copy_w(half, core_slots[half], pos, k)
        core_slots[half] += 1
        go(copy)
        core_list[k].append(copy)

    def begin(k):
        for half in range(2):
            for way in range(2):
                go(ring_copy(half, way, 1, k))
        for half in range(2):
            share(half, here(half), k)

    def last_way(k):
        return 1 if k < 3 else 0

    def advance(way, step, k):
        for half in range(2):
            ring_copy(half, way, step, k).wait_recv()
            if step < 3 or (step == 3 and way == last_way(k)):
                go(ring_copy(half, way, step + 1, k))
            share(half, here(half) - step if way == 0 else here(half) + step, k)

    col = lax.broadcasted_iota(jnp.int32, (1, 256), 1)
    inner = col & (ROWS - 1)
    own_slot = col >> 5
    absolute = jnp.where(inner < STRIP, STRIP * (col >> 4) + inner, -4096)
    turned = ((y + NY + slot_offset(own_slot)) % NY) * 2 + ((col >> 4) & 1)
    relative = jnp.where(inner < STRIP, STRIP * turned + inner, -4096)

    def strip_pick(first, count, target):
        feature = lax.broadcasted_iota(jnp.int32, (count, 256), 0) + first
        return jnp.where(feature == target, 1.0, 0.0).astype(BF16)

    def expand(m):
        low = (208 * m) // 128 * 128
        wide = min(384, D - low)
        exp0[m] = dot(normed[:, low : low + wide], strip_pick(low - 208 * m, wide, absolute)).astype(BF16)
        exp1[m] = dot(normed[:, low : low + wide], strip_pick(low - 208 * m, wide, relative)).astype(BF16)

    def project(k):
        acc[:, 0:CUT] += dot(exp0[(z + NZ + OFFSETS[k]) % NZ], wg0[k].reshape(256, CUT))

    def finish(k):
        for copy in core_list[k]:
            copy.wait_recv()
        for slot in range(*CHUNKS[k]):
            project(slot)

    for half in range(2):
        go(first_copy(half, 1))
        go(first_copy(half, 2))
    for at, entry in enumerate(ROUTE):
        if entry[0] == "start":
            begin(entry[1])
        elif entry[0] == "first":
            for half in range(2):
                first_copy(half, entry[1]).wait_recv()
                if entry[1] <= 5:
                    go(first_copy(half, entry[1] + 2))
        else:
            advance(*entry)
        if at == 0:
            for load in loads[6:9]:
                load.wait()
            values = images[...].astype(F32)
            center = values - jnp.mean(values, axis=-1, keepdims=True)
            spread = jnp.mean(center * center, axis=-1, keepdims=True)
            normed = (center * lax.rsqrt(spread + 1e-06) * attn_gain[...].reshape(1, D)).astype(BF16)
        if 8 <= at < 24 and at % 2 == 0:
            expand((at - 8) // 2)
        if at in (38, 42, 45):
            finish((38, 42, 45).index(at))
    finish(3)
    finish(4)
    for k in range(8):
        part = dot(exp1[k], wg1[k].reshape(256, D - CUT)[:, 0 : 1280 - CUT])
        late = part if k == 0 else late + part
    acc[:, CUT:1280] = late
    lane = lax.broadcasted_iota(jnp.int32, (1, QP), 1)
    keys = acc[:, 384:896].astype(BF16).astype(F32)
    keys = jnp.where((lane >= 32) & (lane < 448), keys, 0.0).astype(BF16)
    vals = acc[:, 768:1280].astype(BF16).astype(F32)

    def sum_copy(h, d):
        return remote(
            summed.at[128 * h : 128 * h + 128, quarter((x + d) % NX)], landed.at[h, d - 1, :, 0:QW],
            x_send.at[h, d - 1], x_recv.at[h, d - 1], xdev(d),
        )

    def tail_copy(h, d):
        return remote(
            summed.at[128 * h : 128 * h + 128, 4 * QW : D], landed.at[h, d - 1, :, QW:QP],
            t_send.at[h, d - 1], t_recv.at[h, d - 1], xdev(d),
        )

    for half_rows in range(2):
        low = 128 * half_rows
        query = pltpu.roll(acc[low : low + 128, 0:512].astype(BF16).astype(F32), 32, 1)
        mixed = jnp.zeros((128, QP), F32)
        for h in range(HEADS_HERE):
            in_q = (lane >= 32 + HEAD_DIM * h) & (lane < 32 + HEAD_DIM * (h + 1))
            in_v = (lane >= 64 + HEAD_DIM * h) & (lane < 64 + HEAD_DIM * (h + 1))
            scores = dot(jnp.where(in_q, query, 0.0).astype(BF16), keys, ((1,), (1,))) * HEAD_DIM ** (-0.5)
            top = jnp.max(scores, axis=-1, keepdims=True)
            grown = jnp.exp(scores - top)
            probs = (grown / jnp.sum(grown, axis=-1, keepdims=True)).astype(BF16)
            mixed += dot(probs, jnp.where(in_v, vals, 0.0).astype(BF16))
        heads = pltpu.roll(mixed.astype(BF16).astype(F32), 32, 1)
        heads = jnp.where(lane >= 96, heads, 0.0).astype(BF16)

        def spread_out(k, carry, low=low, heads=heads):
            weights = wg1[k].reshape(256, D - CUT)[:, 1152 - CUT : D - CUT]
            outp[k, low : low + 128, :] = dot(heads, weights, ((1,), (1,))).astype(BF16)
            return carry

        lax.fori_loop(0, 8, spread_out, 0)
        for t in range(13):
            total = None
            for m in range(128 * t // 208, (128 * t + 127) // 208 + 1):
                term = dot(outp[m, low : low + 128, :], strip_pick(128 * t - 208 * m, 128, relative), ((1,), (1,)))
                total = term if total is None else total + term
            summed[low : low + 128, 128 * t : 128 * t + 128] = total.astype(BF16)
        for d in (2, 1, 3):
            go(sum_copy(half_rows, d))
            pl.when((x + d) % NX == 0)(tail_copy(half_rows, d).start)

    real = (lane < QW) | tail
    own = jnp.concatenate([summed[:, quarter(x)], summed[:, 4 * QW : D]], axis=1).astype(F32)
    base = jnp.concatenate([images[:, quarter(x)], images[:, 4 * QW : D]], axis=1).astype(F32)
    gain = jnp.concatenate([mlp_gain[quarter(x)], mlp_gain[4 * QW : D]]).reshape(1, QP)
    gain = jnp.where(real, gain, 0.0)
    for h in range(2):
        for d in (1, 3, 2):
            sum_copy(h, d).wait_recv()
            pl.when(tail)(tail_copy(h, d).wait_recv)

    attn = own
    for d in (1, 2, 3):
        attn += jnp.concatenate([landed[0, d - 1], landed[1, d - 1]], axis=0).astype(F32)
    residual = jnp.where(real, base + attn, 0.0)

    def width(k):
        return jnp.where(k == 0, 512.0, 384.0).astype(F32)

    mean_here = jnp.sum(residual, axis=-1, keepdims=True) / width(x)
    off = jnp.where(real, residual - mean_here, 0.0)
    dev_here = jnp.sum(off * off, axis=-1, keepdims=True)
    stats[...] = jnp.where(lane128 == 0, mean_here, jnp.where(lane128 == 1, dev_here, 0.0)).T[0:8, :]

    def stat_copy(d):
        return remote(stats, stats_in.at[d - 1], st_send.at[d - 1], st_recv.at[d - 1], xdev(d))

    for d in (2, 1, 3):
        go(stat_copy(d))
    for d in (1, 3, 2):
        stat_copy(d).wait_recv()
    groups = [(stats[...], width(x))] + [(stats_in[d - 1], width((x + NX - d) % NX)) for d in (1, 2, 3)]
    mean = sum(g[0:1, :] * n for g, n in groups) / float(D)
    var = sum(g[1:2, :] + n * (g[0:1, :] - mean) * (g[0:1, :] - mean) for g, n in groups) / float(D)
    scale = lax.rsqrt(var + 1e-06)
    both = jnp.where(row128 == 0, mean, jnp.where(row128 == 1, scale, 0.0)).T
    routed = ((residual - both[:, 0:1]) * both[:, 1:2] * gain).astype(BF16)
    chosen = dot(choosing, routed, ((0,), (0,)))

    def folded(value):
        return jnp.concatenate([value[:, 0:256].reshape(32, 8, 256), value[:, 256:512].reshape(32, 8, 256)], axis=1).astype(BF16)

    def unfolded(value):
        value = value.reshape(32, 16, 256).astype(F32)
        return value[:, 0:8].reshape(256, 256).astype(BF16), value[:, 8:16].reshape(256, 256).astype(BF16)

    picked[...] = folded(chosen)

    def a_copy(i, d):
        to_y, to_z = (y + 2 * i) % NY, (z + d) % NZ
        return remote(
            picked.at[4 * to_z + to_y // 2], arrived.at[pair, z], a_send.at[i, d], a_recv.at[i, d], device(x, to_y, to_z, c)
        )

    for i, d in FAR:
        a_copy(i, d).start()
    arrived[pair, z] = picked[4 * z + pair]

    class Both:
        def __init__(self, main, extra, is_tail):
            self.main, self.extra, self.is_tail = main, extra, is_tail

        def start(self):
            self.main.start()
            pl.when(self.is_tail)(self.extra.start)

        def wait_send(self):
            self.main.wait_send()
            pl.when(self.is_tail)(self.extra.wait_send)

        def wait_recv(self):
            self.main.wait_recv()
            pl.when(self.is_tail)(self.extra.wait_recv)

    def pieces(src_main, dst_main, src_extra, dst_extra, send, recv, target, is_tail):
        return Both(
            remote(src_main, dst_main, send.at[0], recv.at[0], target),
            remote(src_extra, dst_extra, send.at[1], recv.at[1], target),
            is_tail,
        )

    for i, d in FAR[::-1]:
        a_copy(i, d).wait_recv()
    left, right = unfolded(arrived[...])
    rows[par, c, :, quarter(x)] = jnp.concatenate([left, right[:, 0:128]], axis=1)

    @pl.when(tail)
    def _():
        rows[par, c, :, 4 * QW : D] = right[:, 128:256]

    def same(parity, core_index, q_index, send, recv, target, is_tail):
        main = rows.at[parity, core_index, :, quarter(q_index)]
        extra = rows.at[parity, core_index, :, 4 * QW : D]
        return pieces(main, main, extra, extra, send, recv, target, is_tail)

    mate_copy = same(par, c, x, yp_send, yp_recv, mate, tail)
    mate_copy.start()

    def x_copy(k, d):
        parity = par if k == 0 else 1 - par
        return same(parity, c, x, xg_send.at[k, d - 1], xg_recv.at[k, d - 1], xdev(d), tail)

    def x_arrived(k, d):
        from_tail = (x + NX - d) % NX == 0
        parity = par if k == 0 else 1 - par
        return same(parity, c, x, xg_send.at[k, d - 1], xg_recv.at[k, d - 1], xdev(d), from_tail)

    def core_copy(k, d):
        from_x = (x + NX - d) % NX
        parity = par if k == 0 else 1 - par
        return same(parity, c, from_x, cg_send.at[k, d], cg_recv.at[k, d], core, from_x == 0)

    for d in (2, 1, 3):
        x_copy(0, d).start()
    core_copy(0, 0).start()
    mate_copy.wait_recv()
    for d in (2, 1, 3):
        x_copy(1, d).start()
    core_copy(1, 0).start()
    for d in (1, 3, 2):
        x_arrived(0, d).wait_recv()
        core_copy(0, d).start()
    for load in loads[9:]:
        load.wait()

    def expert(parity, core_index):
        hidden = gelu_tanh(dot(rows[parity, core_index], w_in[...])).astype(BF16)
        parts[parity, core_index] = dot(hidden, w_out[...]).astype(BF16)

    def r1_copy(k):
        parity = par if k == 0 else 1 - par
        return remote(parts.at[parity, 1 - c], r1.at[parity], r1_send.at[k], r1_recv.at[k], core)

    for d in range(4):
        core_copy(0, d).wait_recv()
    expert(par, 1 - c)
    r1_copy(0).start()
    expert(par, c)
    for d in (1, 3, 2):
        x_arrived(1, d).wait_recv()
        core_copy(1, d).start()

    def both_cores(parity):
        q[parity] = (parts[parity, c].astype(F32) + r1[parity].astype(F32)).astype(BF16)

    def quarters(src, rows_of, dst, send, recv, d):
        to = (x + d) % NX
        return pieces(
            src.at[rows_of, quarter(to)], dst.at[d - 1, :, 0:QW], src.at[rows_of, 4 * QW : D], dst.at[d - 1, :, QW:QP],
            send.at[d - 1], recv.at[d - 1], xdev(d), to == 0,
        )

    def got(copy):
        copy.main.wait_recv()
        pl.when(tail)(copy.extra.wait_recv)

    def own_sum_copy(d):
        return quarters(q.at[par], pl.ds(0, FIRST), r2a, r2_send, r2_recv, d)

    def mate_sum_copy(d):
        return quarters(q.at[1 - par], pl.ds(0, FIRST), r2c, r2c_send, r2c_recv, d)

    def rest_copy():
        return remote(q.at[1 - par, FIRST:256], r2b, r2y_send, r2y_recv, mate)

    def late_copy(d):
        return quarters(sb, pl.ds(0, 256 - FIRST), r3b, r3_send, r3_recv, d)

    def summed_copy():
        return remote(sa, r3a, r3y_send, r3y_recv, mate)

    def mine_of(value):
        return jnp.concatenate([value[:, quarter(x)], value[:, 4 * QW : D]], axis=1).astype(F32)

    r1_copy(0).wait_recv()
    both_cores(par)
    for d in (2, 1, 3):
        own_sum_copy(d).start()
    for d in range(4):
        core_copy(1, d).wait_recv()
    expert(1 - par, 1 - c)
    r1_copy(1).start()
    expert(1 - par, c)
    r1_copy(1).wait_recv()
    both_cores(1 - par)
    rest_copy().start()
    for d in (2, 1, 3):
        mate_sum_copy(d).start()
    for d in (1, 3, 2):
        got(own_sum_copy(d))
    own_total = mine_of(q.at[par, 0:FIRST])
    for d in (1, 2, 3):
        own_total += r2a[d - 1].astype(F32)
    rest_copy().wait_recv()
    sb[...] = (q[par, FIRST:256].astype(F32) + r2b[...].astype(F32)).astype(BF16)
    for d in (2, 1, 3):
        late_copy(d).start()
    for d in (1, 3, 2):
        got(mate_sum_copy(d))
    total = mine_of(q.at[1 - par, 0:FIRST])
    for d in (1, 2, 3):
        total += r2c[d - 1].astype(F32)
    sa[...] = jnp.where(real, total, 0.0).astype(BF16)
    summed_copy().start()
    total = mine_of(sb)
    for d in (1, 3, 2):
        got(late_copy(d))
        total += r3b[d - 1].astype(F32)
    low_rows = jnp.where(real, total, 0.0)
    summed_copy().wait_recv()
    result = jnp.concatenate([jnp.where(real, own_total + r3a[...].astype(F32), 0.0), low_rows], axis=0)

    returning[...] = folded(result).reshape(4, 8, 16, 256)

    def aa_copy(i, d):
        to_y, to_z = (y + 2 * i) % NY, (z + d) % NZ
        return remote(
            returning.at[to_y // 2, to_z], home.at[4 * z + pair], aa_send.at[i, d], aa_recv.at[i, d], device(x, to_y, to_z, c)
        )

    for i, d in FAR:
        aa_copy(i, d).start()
    home[4 * z + pair] = returning[pair, z]
    for i, d in FAR[::-1]:
        aa_copy(i, d).wait_recv()
    left, right = unfolded(home[...])
    final[...] = (residual + jnp.concatenate([dot(placing, left), dot(placing, right)], axis=1)).astype(BF16)

    def f_copy(d):
        to = pl.ds(pl.multiple_of((x + d) % NX * 64, 64), 64)
        return pieces(
            final.at[to, 0:QW], gathered.at[:, quarter(x)],
            final.at[to, QW:QP], gathered.at[:, 4 * QW : D],
            f_send.at[d - 1], f_recv.at[d - 1], xdev(d), tail,
        )

    for d in (2, 1, 3):
        f_copy(d).start()
    mine = pl.ds(pl.multiple_of(x * 64, 64), 64)
    gathered[:, quarter(x)] = final[mine, 0:QW]

    @pl.when(tail)
    def _():
        gathered[:, 4 * QW : D] = final[mine, QW:QP]

    for d in (1, 3, 2):
        copy = f_copy(d)
        copy.main.wait_recv()
        pl.when((x + NX - d) % NX == 0)(copy.extra.wait_recv)
    out[...] = gathered[...]

    for copy in started:
        copy.wait_send()
    for h in range(2):
        for d in (1, 2, 3):
            pl.when((x + d) % NX == 0)(tail_copy(h, d).wait_send)
    for i, d in FAR:
        a_copy(i, d).wait_send()
        aa_copy(i, d).wait_send()
    mate_copy.wait_send()
    for k in range(2):
        for d in (1, 2, 3):
            x_copy(k, d).wait_send()
        for d in range(4):
            core_copy(k, d).wait_send()
        r1_copy(k).wait_send()
    for d in (1, 2, 3):
        own_sum_copy(d).wait_send()
        mate_sum_copy(d).wait_send()
        late_copy(d).wait_send()
        f_copy(d).wait_send()
    rest_copy().wait_send()
    summed_copy().wait_send()


def block(images, attn_gain, mlp_gain, qkv, proj_t, ids_t, gates_t, kept, counts, w_in, w_out):
    sem = pltpu.SemaphoreType.DMA
    vm = pl.BlockSpec(memory_space=pltpu.VMEM)
    hbm = pl.BlockSpec(memory_space=pl.ANY)

    def v(*shape, kind=BF16):
        return pltpu.VMEM(shape, kind)

    return pl.pallas_call(
        block_kernel,
        name="block",
        out_shape=jax.ShapeDtypeStruct((64, D), BF16),
        in_specs=[hbm] * 11,
        out_specs=vm,
        scratch_shapes=[
            v(PATCHES, D), v(D, kind=F32), v(D, kind=F32), v(3, STRIP, 416), v(STRIP, 416),
            v(2, PATCHES, kind=jnp.int32), v(2, PATCHES), v(8, EXPERTS, kind=jnp.int32), v(1, EXPERTS, kind=jnp.int32),
            v(8, NY, 2, ROWS, CUT), v(NZ, 8, 2, ROWS, D - CUT), v(4, ROWS, D, kind=F32),
            v(8, PATCHES, 256), v(8, PATCHES, 256), v(PATCHES, 1280, kind=F32), v(8, PATCHES, 256), v(PATCHES, D),
            v(2, 3, 128, QP), v(8, 256, kind=F32), v(3, 8, 256, kind=F32),
            v(D, 512), v(512, D), v(32, 16, 256), v(4, 8, 16, 256), v(2, 2, 256, D), v(2, 2, 256, D), v(2, 256, D),
            v(2, 256, D), v(3, FIRST, QP), v(3, FIRST, QP), v(256 - FIRST, D), v(FIRST, QP), v(256 - FIRST, D), v(FIRST, QP), v(3, 256 - FIRST, QP),
            v(4, 8, 16, 256), v(32, 16, 256), v(256, QP), v(64, D),
            sem((2, 7)), sem((2, 7)), sem((2, 2, 20)), sem((2, 2, 20)), sem((2, 40)), sem((2, 40)),
            sem((2, 3)), sem((2, 3)), sem((2, 3)), sem((2, 3)), sem((3,)), sem((3,)),
            sem((11,)), sem((4, 8)), sem((4, 8)), sem((2,)), sem((2,)),
            sem((2, 3, 2)), sem((2, 3, 2)), sem((2, 4, 2)), sem((2, 4, 2)),
            sem((2,)), sem((2,)), sem((3, 2)), sem((3, 2)), sem((3, 2)), sem((3, 2)), sem, sem, sem((3, 2)), sem((3, 2)), sem, sem,
            sem((4, 8)), sem((4, 8)), sem((3, 2)), sem((3, 2)),
        ],
        compiler_params=pltpu.CompilerParams(collective_id=1, has_side_effects=True, vmem_limit_bytes=56 << 20),
    )(images, attn_gain, mlp_gain, qkv, proj_t, ids_t, gates_t, kept, counts, w_in, w_out)


def on_device(
    images, attn_gain, qkv_weight, proj_weight, mlp_gain, expert_in, expert_out,
    gate_values, expert_ids, kept_patches, kept_counts,
):
    return block(
        images, attn_gain, mlp_gain, qkv_weight, proj_weight.T, expert_ids.T, gate_values.T,
        kept_patches[0].T, kept_counts, expert_in, expert_out,
    )


def solution(mesh):
    placed = (
        P("dp", None), P(), P(None, "dp", "mp"), P("mp", "dp"), P(), P(None, ("dp", "mp")), P(("dp", "mp"), None),
        P("dp", None), P("dp", None), P("dp", None, None), P("dp", None),
    )
    return jax.shard_map(on_device, mesh=mesh, in_specs=placed, out_specs=P(("dp", "mp"), None), check_vma=False)
```

time: 156 us -> 140 us (0.90)
  the two profiles are of different devices: /device:TPU:10 before, /device:TPU:2 now
where the time goes in v3:
time: 140 us
  Pallas kernels  138 us (99%)
  local copies, waits for them, and re-layouts  1.63 us (1%)
    pallas_call x1, Pallas kernels, block(): pl.pallas_call(block_kernel, name='block', out_shape=jax.ShapeDtypeStruct...  138 us

profile of v3, /device:TPU:2, one launch (start us, length us, event | category | flops | bytes accessed | tf_op | source)
XLA Modules:
  0.0 139.7 jit_solution(16368270320106042542)
XLA Ops:
  0.0 138.1 %block.1 = bf16[64,1664]{1,0:T(8,128)(2,1)} custom-call(bf16[256,1664]{1,0:T(8,128)(2,1)} %images_hbm.1, f32[1664]{0:T(1024)} %attn_gain_hbm.1, f32[1664]{0:T(1024)} %mlp_gain_hbm.1, bf16[3,13,416]{2,1,0:T(8,128)(2,1)} %qkv_hbm.1, bf16[13,416]{1,0:T(8,128)(2,1)} %bitcast.6, s32[2,256]{1,0:T(2,128)} %bitcast.8, bf16[2,256]{1,0:T(2,128)(2,1)} %bitcast.9, ...), custom_call_target="tpu_custom_call" | custom-call | tf_op jit(solution)/shard_map/block/pallas_call | solution.py:607
  138.1 1.6 %copy.13 = bf16[64,1664]{1,0:T(8,128)(2,1)} copy(bf16[64,1664]{1,0:T(8,128)(2,1)} %block.1) | data formatting | bytes 425984

commit v4 on v3

--- a/solution.py
+++ b/solution.py
@@ -53,7 +53,8 @@
 
 
 FAR = sorted(((i, d) for i in range(4) for d in range(8) if (i, d) != (0, 0)), key=lambda s: -(min(2 * s[0], 8 - 2 * s[0]) + min(s[1], 8 - s[1])))
-FIRST = 176
+FIRST = 160
+HALF = FIRST // 2
 CUT = 896
 OFFSETS = (0, 1, -1, 2, -2, 3, -3, 4)
 CHUNKS = ((0, 1), (1, 3), (3, 5), (5, 7), (7, 8))
@@ -74,9 +75,9 @@
     images_hbm, attn_gain_hbm, mlp_gain_hbm, qkv_hbm, proj_hbm, ids_hbm, gates_hbm, kept_hbm, counts_hbm,
     w_in_hbm, w_out_hbm, out,
     images, attn_gain, mlp_gain, qkv, proj, ids_t, gates_t, kept, counts,
-    wg0, wg1, scratch_strip, exp0, exp1, acc, outp, summed, landed, stats, stats_in,
+    wg0, wg1, scratch_strip, exp0, exp1, acc, outp, summed, landed,
     w_in, w_out, picked, arrived, rows, parts, r1, q, r2a, r2c, r2b, sa, sb, r3a, r3b, returning, home, final, gathered,
-    s1_send, s1_recv, ring_send, ring_recv, core_send, core_recv, x_send, x_recv, t_send, t_recv, st_send, st_recv,
+    s1_send, s1_recv, ring_send, ring_recv, core_send, core_recv, x_send, x_recv, t_send, t_recv,
     w_sem, a_send, a_recv, yp_send, yp_recv, xg_send, xg_recv, cg_send, cg_recv,
     r1_send, r1_recv, r2_send, r2_recv, r2c_send, r2c_recv, r2y_send, r2y_recv, r3_send, r3_recv, r3y_send, r3y_recv,
     aa_send, aa_recv, f_send, f_recv,
@@ -261,7 +262,8 @@
             for load in loads[6:9]:
                 load.wait()
             values = images[...].astype(F32)
-            center = values - jnp.mean(values, axis=-1, keepdims=True)
+            image_mean = jnp.mean(values, axis=-1, keepdims=True)
+            center = values - image_mean
             spread = jnp.mean(center * center, axis=-1, keepdims=True)
             normed = (center * lax.rsqrt(spread + 1e-06) * attn_gain[...].reshape(1, D)).astype(BF16)
         if 8 <= at < 24 and at % 2 == 0:
@@ -276,7 +278,7 @@
     acc[:, CUT:1280] = late
     lane = lax.broadcasted_iota(jnp.int32, (1, QP), 1)
     keys = acc[:, 384:896].astype(BF16).astype(F32)
-    keys = jnp.where((lane >= 32) & (lane < 448), keys, 0.0).astype(BF16)
+    keys = jnp.where((lane >= 32) & (lane < 448), keys, 0.0).T.astype(BF16)
     vals = acc[:, 768:1280].astype(BF16).astype(F32)
 
     def sum_copy(h, d):
@@ -298,26 +300,26 @@
         for h in range(HEADS_HERE):
             in_q = (lane >= 32 + HEAD_DIM * h) & (lane < 32 + HEAD_DIM * (h + 1))
             in_v = (lane >= 64 + HEAD_DIM * h) & (lane < 64 + HEAD_DIM * (h + 1))
-            scores = dot(jnp.where(in_q, query, 0.0).astype(BF16), keys, ((1,), (1,))) * HEAD_DIM ** (-0.5)
+            scores = dot(jnp.where(in_q, query, 0.0).astype(BF16), keys) * HEAD_DIM ** (-0.5)
             top = jnp.max(scores, axis=-1, keepdims=True)
             grown = jnp.exp(scores - top)
             probs = (grown / jnp.sum(grown, axis=-1, keepdims=True)).astype(BF16)
             mixed += dot(probs, jnp.where(in_v, vals, 0.0).astype(BF16))
         heads = pltpu.roll(mixed.astype(BF16).astype(F32), 32, 1)
-        heads = jnp.where(lane >= 96, heads, 0.0).astype(BF16)
+        heads = jnp.where(lane >= 96, heads, 0.0).T.astype(BF16)
 
         def spread_out(k, carry, low=low, heads=heads):
             weights = wg1[k].reshape(256, D - CUT)[:, 1152 - CUT : D - CUT]
-            outp[k, low : low + 128, :] = dot(heads, weights, ((1,), (1,))).astype(BF16)
+            outp[k, :, low : low + 128] = dot(weights, heads).astype(BF16)
             return carry
 
         lax.fori_loop(0, 8, spread_out, 0)
         for t in range(13):
             total = None
             for m in range(128 * t // 208, (128 * t + 127) // 208 + 1):
-                term = dot(outp[m, low : low + 128, :], strip_pick(128 * t - 208 * m, 128, relative), ((1,), (1,)))
+                term = dot(strip_pick(128 * t - 208 * m, 128, relative), outp[m, :, low : low + 128])
                 total = term if total is None else total + term
-            summed[low : low + 128, 128 * t : 128 * t + 128] = total.astype(BF16)
+            summed[low : low + 128, 128 * t : 128 * t + 128] = total.T.astype(BF16)
         for d in (2, 1, 3):
             go(sum_copy(half_rows, d))
             pl.when((x + d) % NX == 0)(tail_copy(half_rows, d).start)
@@ -325,8 +327,6 @@
     real = (lane < QW) | tail
     own = jnp.concatenate([summed[:, quarter(x)], summed[:, 4 * QW : D]], axis=1).astype(F32)
     base = jnp.concatenate([images[:, quarter(x)], images[:, 4 * QW : D]], axis=1).astype(F32)
-    gain = jnp.concatenate([mlp_gain[quarter(x)], mlp_gain[4 * QW : D]]).reshape(1, QP)
-    gain = jnp.where(real, gain, 0.0)
     for h in range(2):
         for d in (1, 3, 2):
             sum_copy(h, d).wait_recv()
@@ -337,27 +337,7 @@
         attn += jnp.concatenate([landed[0, d - 1], landed[1, d - 1]], axis=0).astype(F32)
     residual = jnp.where(real, base + attn, 0.0)
 
-    def width(k):
-        return jnp.where(k == 0, 512.0, 384.0).astype(F32)
-
-    mean_here = jnp.sum(residual, axis=-1, keepdims=True) / width(x)
-    off = jnp.where(real, residual - mean_here, 0.0)
-    dev_here = jnp.sum(off * off, axis=-1, keepdims=True)
-    stats[...] = jnp.where(lane128 == 0, mean_here, jnp.where(lane128 == 1, dev_here, 0.0)).T[0:8, :]
-
-    def stat_copy(d):
-        return remote(stats, stats_in.at[d - 1], st_send.at[d - 1], st_recv.at[d - 1], xdev(d))
-
-    for d in (2, 1, 3):
-        go(stat_copy(d))
-    for d in (1, 3, 2):
-        stat_copy(d).wait_recv()
-    groups = [(stats[...], width(x))] + [(stats_in[d - 1], width((x + NX - d) % NX)) for d in (1, 2, 3)]
-    mean = sum(g[0:1, :] * n for g, n in groups) / float(D)
-    var = sum(g[1:2, :] + n * (g[0:1, :] - mean) * (g[0:1, :] - mean) for g, n in groups) / float(D)
-    scale = lax.rsqrt(var + 1e-06)
-    both = jnp.where(row128 == 0, mean, jnp.where(row128 == 1, scale, 0.0)).T
-    routed = ((residual - both[:, 0:1]) * both[:, 1:2] * gain).astype(BF16)
+    routed = jnp.where(real, residual - image_mean, 0.0).astype(BF16)
     chosen = dot(choosing, routed, ((0,), (0,)))
 
     def folded(value):
@@ -411,65 +391,109 @@
     def _():
         rows[par, c, :, 4 * QW : D] = right[:, 128:256]
 
-    def same(parity, core_index, q_index, send, recv, target, is_tail):
-        main = rows.at[parity, core_index, :, quarter(q_index)]
-        extra = rows.at[parity, core_index, :, 4 * QW : D]
-        return pieces(main, main, extra, extra, send, recv, target, is_tail)
-
-    mate_copy = same(par, c, x, yp_send, yp_recv, mate, tail)
-    mate_copy.start()
-
-    def x_copy(k, d):
-        parity = par if k == 0 else 1 - par
-        return same(parity, c, x, xg_send.at[k, d - 1], xg_recv.at[k, d - 1], xdev(d), tail)
-
-    def x_arrived(k, d):
-        from_tail = (x + NX - d) % NX == 0
-        parity = par if k == 0 else 1 - par
-        return same(parity, c, x, xg_send.at[k, d - 1], xg_recv.at[k, d - 1], xdev(d), from_tail)
-
-    def core_copy(k, d):
-        from_x = (x + NX - d) % NX
-        parity = par if k == 0 else 1 - par
-        return same(parity, c, from_x, cg_send.at[k, d], cg_recv.at[k, d], core, from_x == 0)
-
-    for d in (2, 1, 3):
-        x_copy(0, d).start()
-    core_copy(0, 0).start()
-    mate_copy.wait_recv()
-    for d in (2, 1, 3):
-        x_copy(1, d).start()
-    core_copy(1, 0).start()
-    for d in (1, 3, 2):
-        x_arrived(0, d).wait_recv()
-        core_copy(0, d).start()
-    for load in loads[9:]:
-        load.wait()
+    def same(parity, q_index, low, high, send, recv, target):
+        main = rows.at[parity, c, low:high, quarter(q_index)]
+        extra = rows.at[parity, c, low:high, 4 * QW : D]
+        return pieces(main, main, extra, extra, send, recv, target, q_index == 0)
+
+    def cut(which, j):
+        return ((0, 128), (128, 256))[j] if which == 0 else ((0, 64), (64, 128))[j]
+
+    def x_piece(which, way, j, q_index):
+        low, high = cut(which, way if j == 2 else j)
+        return same(
+            par if which == 0 else 1 - par, q_index, low, high,
+            xg_send.at[which, way, j], xg_recv.at[which, way, j], xdev(1 if way == 0 else 3),
+        )
+
+    def x_from(way, j):
+        hops = 2 if j == 2 else 1
+        return (x + NX - hops) % NX if way == 0 else (x + hops) % NX
+
+    def y_piece(j, parity):
+        low, high = (0, 128) if j == 0 else (128, 256)
+        q_index = (x + (0, 0, NX - 1, 1, 2)[j]) % NX
+        return same(parity, q_index, low, high, yp_send.at[j], yp_recv.at[j], mate)
+
+    group_sent, to_core = [], ([], [])
+
+    def put(copy):
+        copy.start()
+        group_sent.append(copy)
+
+    def over(which, q_index, low, high):
+        index = len(to_core[0]) + len(to_core[1])
+        copy = same(par if which == 0 else 1 - par, q_index, low, high, cg_send.at[index], cg_recv.at[index], core)
+        put(copy)
+        to_core[which].append(copy)
+
+    def take_x(which, way, j):
+        q_index = x_from(way, j)
+        x_piece(which, way, j, q_index).wait_recv()
+        if j == way:
+            put(x_piece(which, way, 2, q_index))
+        if which == 0 and (way, j) in ((0, 1), (1, 1), (1, 2)):
+            put(y_piece({(0, 1): 2, (1, 1): 3, (1, 2): 4}[way, j], par))
+        over(which, q_index, *cut(which, way if j == 2 else j))
+
+    def send_x(which):
+        for way, j in ((0, 0), (1, 1), (0, 1), (1, 0)):
+            put(x_piece(which, way, j, x))
+
+    def take_y(j):
+        y_piece(j, 1 - par).wait_recv()
+        if j == 0:
+            send_x(1)
+        over(1, (x + (0, 0, NX - 1, 1, 2)[j]) % NX, *((0, 128) if j == 0 else (128, 256)))
+
+    send_x(0)
+    put(y_piece(0, par))
+    put(y_piece(1, par))
+    over(0, x, 0, 256)
 
     def expert(parity, core_index):
-        hidden = gelu_tanh(dot(rows[parity, core_index], w_in[...])).astype(BF16)
+        values = rows[parity, core_index].astype(F32)
+        center = values - jnp.mean(values, axis=-1, keepdims=True)
+        spread = jnp.mean(center * center, axis=-1, keepdims=True)
+        normed = (center * lax.rsqrt(spread + 1e-06) * mlp_gain[...].reshape(1, D)).astype(BF16)
+        hidden = gelu_tanh(dot(normed, w_in[...])).astype(BF16)
         parts[parity, core_index] = dot(hidden, w_out[...]).astype(BF16)
 
     def r1_copy(k):
         parity = par if k == 0 else 1 - par
         return remote(parts.at[parity, 1 - c], r1.at[parity], r1_send.at[k], r1_recv.at[k], core)
 
-    for d in range(4):
-        core_copy(0, d).wait_recv()
+    take_x(0, 0, 0)
+    take_x(0, 1, 1)
+    take_y(0)
+    take_x(0, 0, 1)
+    take_x(0, 1, 0)
+    take_y(1)
+    take_x(0, 0, 2)
+    take_x(0, 1, 2)
+    take_x(1, 0, 0)
+    take_x(1, 1, 1)
+    for load in loads[9:]:
+        load.wait()
+    for copy in to_core[0]:
+        copy.wait_recv()
     expert(par, 1 - c)
     r1_copy(0).start()
+    take_x(1, 0, 1)
+    take_x(1, 1, 0)
+    take_y(3)
+    take_y(2)
     expert(par, c)
-    for d in (1, 3, 2):
-        x_arrived(1, d).wait_recv()
-        core_copy(1, d).start()
-
+    take_x(1, 0, 2)
+    take_x(1, 1, 2)
+    take_y(4)
     def both_cores(parity):
         q[parity] = (parts[parity, c].astype(F32) + r1[parity].astype(F32)).astype(BF16)
 
-    def quarters(src, rows_of, dst, send, recv, d):
+    def quarters(src, rows_of, rows_to, dst, send, recv, d):
         to = (x + d) % NX
         return pieces(
-            src.at[rows_of, quarter(to)], dst.at[d - 1, :, 0:QW], src.at[rows_of, 4 * QW : D], dst.at[d - 1, :, QW:QP],
+            src.at[rows_of, quarter(to)], dst.at[d - 1, rows_to, 0:QW], src.at[rows_of, 4 * QW : D], dst.at[d - 1, rows_to, QW:QP],
             send.at[d - 1], recv.at[d - 1], xdev(d), to == 0,
         )
 
@@ -478,19 +502,21 @@
         pl.when(tail)(copy.extra.wait_recv)
 
     def own_sum_copy(d):
-        return quarters(q.at[par], pl.ds(0, FIRST), r2a, r2_send, r2_recv, d)
-
-    def mate_sum_copy(d):
-        return quarters(q.at[1 - par], pl.ds(0, FIRST), r2c, r2c_send, r2c_recv, d)
+        return quarters(q.at[par], pl.ds(0, FIRST), pl.ds(0, FIRST), r2a, r2_send, r2_recv, d)
+
+    def mate_sum_copy(i, d):
+        part = pl.ds(i * HALF, HALF)
+        return quarters(q.at[1 - par], part, part, r2c, r2c_send.at[i], r2c_recv.at[i], d)
 
     def rest_copy():
         return remote(q.at[1 - par, FIRST:256], r2b, r2y_send, r2y_recv, mate)
 
     def late_copy(d):
-        return quarters(sb, pl.ds(0, 256 - FIRST), r3b, r3_send, r3_recv, d)
-
-    def summed_copy():
-        return remote(sa, r3a, r3y_send, r3y_recv, mate)
+        return quarters(sb, pl.ds(0, 256 - FIRST), pl.ds(0, 256 - FIRST), r3b, r3_send, r3_recv, d)
+
+    def summed_copy(i):
+        part = pl.ds(i * HALF, HALF)
+        return remote(sa.at[part], r3a.at[part], r3y_send.at[i], r3y_recv.at[i], mate)
 
     def mine_of(value):
         return jnp.concatenate([value[:, quarter(x)], value[:, 4 * QW : D]], axis=1).astype(F32)
@@ -499,39 +525,47 @@
     both_cores(par)
     for d in (2, 1, 3):
         own_sum_copy(d).start()
-    for d in range(4):
-        core_copy(1, d).wait_recv()
+    for copy in to_core[1]:
+        copy.wait_recv()
     expert(1 - par, 1 - c)
     r1_copy(1).start()
     expert(1 - par, c)
     r1_copy(1).wait_recv()
     both_cores(1 - par)
     rest_copy().start()
-    for d in (2, 1, 3):
-        mate_sum_copy(d).start()
+    for i in range(2):
+        for d in (2, 1, 3):
+            mate_sum_copy(i, d).start()
     for d in (1, 3, 2):
         got(own_sum_copy(d))
     own_total = mine_of(q.at[par, 0:FIRST])
     for d in (1, 2, 3):
         own_total += r2a[d - 1].astype(F32)
+
+    def pass_on(i):
+        for d in (1, 3, 2):
+            got(mate_sum_copy(i, d))
+        low, high = i * HALF, (i + 1) * HALF
+        total = mine_of(q.at[1 - par, low:high])
+        for d in (1, 2, 3):
+            total += r2c[d - 1, low:high].astype(F32)
+        sa[low:high] = jnp.where(real, total, 0.0).astype(BF16)
+        summed_copy(i).start()
+
+    pass_on(0)
     rest_copy().wait_recv()
     sb[...] = (q[par, FIRST:256].astype(F32) + r2b[...].astype(F32)).astype(BF16)
     for d in (2, 1, 3):
         late_copy(d).start()
-    for d in (1, 3, 2):
-        got(mate_sum_copy(d))
-    total = mine_of(q.at[1 - par, 0:FIRST])
-    for d in (1, 2, 3):
-        total += r2c[d - 1].astype(F32)
-    sa[...] = jnp.where(real, total, 0.0).astype(BF16)
-    summed_copy().start()
+    pass_on(1)
     total = mine_of(sb)
+    summed_copy(0).wait_recv()
+    summed_copy(1).wait_recv()
+    high_rows = jnp.where(real, own_total + r3a[...].astype(F32), 0.0)
     for d in (1, 3, 2):
         got(late_copy(d))
         total += r3b[d - 1].astype(F32)
-    low_rows = jnp.where(real, total, 0.0)
-    summed_copy().wait_recv()
-    result = jnp.concatenate([jnp.where(real, own_total + r3a[...].astype(F32), 0.0), low_rows], axis=0)
+    result = jnp.concatenate([high_rows, jnp.where(real, total, 0.0)], axis=0)
 
     returning[...] = folded(result).reshape(4, 8, 16, 256)
 
@@ -580,20 +614,19 @@
     for i, d in FAR:
         a_copy(i, d).wait_send()
         aa_copy(i, d).wait_send()
-    mate_copy.wait_send()
+    for copy in group_sent:
+        copy.wait_send()
     for k in range(2):
-        for d in (1, 2, 3):
-            x_copy(k, d).wait_send()
-        for d in range(4):
-            core_copy(k, d).wait_send()
         r1_copy(k).wait_send()
     for d in (1, 2, 3):
         own_sum_copy(d).wait_send()
-        mate_sum_copy(d).wait_send()
+        mate_sum_copy(0, d).wait_send()
+        mate_sum_copy(1, d).wait_send()
         late_copy(d).wait_send()
         f_copy(d).wait_send()
     rest_copy().wait_send()
-    summed_copy().wait_send()
+    summed_copy(0).wait_send()
+    summed_copy(1).wait_send()
 
 
 def block(images, attn_gain, mlp_gain, qkv, proj_t, ids_t, gates_t, kept, counts, w_in, w_out):
@@ -615,15 +648,15 @@
             v(2, PATCHES, kind=jnp.int32), v(2, PATCHES), v(8, EXPERTS, kind=jnp.int32), v(1, EXPERTS, kind=jnp.int32),
             v(8, NY, 2, ROWS, CUT), v(NZ, 8, 2, ROWS, D - CUT), v(4, ROWS, D, kind=F32),
             v(8, PATCHES, 256), v(8, PATCHES, 256), v(PATCHES, 1280, kind=F32), v(8, PATCHES, 256), v(PATCHES, D),
-            v(2, 3, 128, QP), v(8, 256, kind=F32), v(3, 8, 256, kind=F32),
+            v(2, 3, 128, QP),
             v(D, 512), v(512, D), v(32, 16, 256), v(4, 8, 16, 256), v(2, 2, 256, D), v(2, 2, 256, D), v(2, 256, D),
             v(2, 256, D), v(3, FIRST, QP), v(3, FIRST, QP), v(256 - FIRST, D), v(FIRST, QP), v(256 - FIRST, D), v(FIRST, QP), v(3, 256 - FIRST, QP),
             v(4, 8, 16, 256), v(32, 16, 256), v(256, QP), v(64, D),
             sem((2, 7)), sem((2, 7)), sem((2, 2, 20)), sem((2, 2, 20)), sem((2, 40)), sem((2, 40)),
-            sem((2, 3)), sem((2, 3)), sem((2, 3)), sem((2, 3)), sem((3,)), sem((3,)),
-            sem((11,)), sem((4, 8)), sem((4, 8)), sem((2,)), sem((2,)),
-            sem((2, 3, 2)), sem((2, 3, 2)), sem((2, 4, 2)), sem((2, 4, 2)),
-            sem((2,)), sem((2,)), sem((3, 2)), sem((3, 2)), sem((3, 2)), sem((3, 2)), sem, sem, sem((3, 2)), sem((3, 2)), sem, sem,
+            sem((2, 3)), sem((2, 3)), sem((2, 3)), sem((2, 3)),
+            sem((11,)), sem((4, 8)), sem((4, 8)), sem((5, 2)), sem((5, 2)),
+            sem((2, 2, 3, 2)), sem((2, 2, 3, 2)), sem((18, 2)), sem((18, 2)),
+            sem((2,)), sem((2,)), sem((3, 2)), sem((3, 2)), sem((2, 3, 2)), sem((2, 3, 2)), sem, sem, sem((3, 2)), sem((3, 2)), sem((2,)), sem((2,)),
             sem((4, 8)), sem((4, 8)), sem((3, 2)), sem((3, 2)),
         ],
         compiler_params=pltpu.CompilerParams(collective_id=1, has_side_effects=True, vmem_limit_bytes=56 << 20),

time: 140 us -> 129 us (0.921)
  the two profiles are of different devices: /device:TPU:2 before, /device:TPU:10 now
where the time goes in v4:
time: 129 us
  Pallas kernels  127 us (98%)
  local copies, waits for them, and re-layouts  1.63 us (1%)
    pallas_call x1, Pallas kernels, block(): pl.pallas_call(block_kernel, name='block', out_shape=jax.ShapeDtypeStruct...  127 us

profile of v4, /device:TPU:10, one launch (start us, length us, event | category | flops | bytes accessed | tf_op | source)
XLA Modules:
  0.0 129.1 jit_solution(15260209544924347211)
XLA Ops:
  0.0 127.4 %block.1 = bf16[64,1664]{1,0:T(8,128)(2,1)} custom-call(bf16[256,1664]{1,0:T(8,128)(2,1)} %images_hbm.1, f32[1664]{0:T(1024)} %attn_gain_hbm.1, f32[1664]{0:T(1024)} %mlp_gain_hbm.1, bf16[3,13,416]{2,1,0:T(8,128)(2,1)} %qkv_hbm.1, bf16[13,416]{1,0:T(8,128)(2,1)} %bitcast.6, s32[2,256]{1,0:T(2,128)} %bitcast.8, bf16[2,256]{1,0:T(2,128)(2,1)} %bitcast.9, ...), custom_call_target="tpu_custom_call" | custom-call | tf_op jit(solution)/shard_map/block/pallas_call | solution.py:640
  127.5 1.6 %copy.13 = bf16[64,1664]{1,0:T(8,128)(2,1)} copy(bf16[64,1664]{1,0:T(8,128)(2,1)} %block.1) | data formatting | bytes 425984

commit v5 on v4

--- a/solution.py
+++ b/solution.py
@@ -164,7 +164,7 @@
         else:
             src, dst = wg1.at[z, source, c], wg1.at[z, slot, c]
         return remote(
-            src, dst, s1_send.at[half, slot - 1], s1_recv.at[half, slot - 1], ring(half, 1, -1 if slot % 2 else 1)
+            src, dst, s1_send.at[half], s1_recv.at[half, slot - 1], ring(half, 1, -1 if slot % 2 else 1)
         )
 
     def chunk_ref(half, pos, k):
@@ -181,31 +181,26 @@
         piece = chunk_ref(half, pos + 8, k)
         index = (step - 1) * 5 + k
         return remote(
-            piece, piece, ring_send.at[half, way, index], ring_recv.at[half, way, index], ring(half, 2, 1 if way == 0 else -1)
-        )
-
-    def core_copy_w(half, slot, pos, k):
+            piece, piece, ring_send.at[half], ring_recv.at[half, way, index], ring(half, 2, 1 if way == 0 else -1)
+        )
+
+    def core_copy_w(half, pos, k):
         piece = chunk_ref(half, pos + 8, k)
-        return remote(piece, piece, core_send.at[half, slot], core_recv.at[half, slot], core)
-
-    started, core_list = [], [[] for _ in CHUNKS]
+        return remote(piece, piece, core_send.at[half], core_recv.at[half, k], core)
+
+    def share(half, pos, k):
+        core_copy_w(half, pos, k).start()
+
+    started = []
 
     def go(copy):
         copy.start()
         started.append(copy)
 
-    core_slots = [0, 0]
-
-    def share(half, pos, k):
-        copy = core_copy_w(half, core_slots[half], pos, k)
-        core_slots[half] += 1
-        go(copy)
-        core_list[k].append(copy)
-
     def begin(k):
         for half in range(2):
             for way in range(2):
-                go(ring_copy(half, way, 1, k))
+                ring_copy(half, way, 1, k).start()
         for half in range(2):
             share(half, here(half), k)
 
@@ -216,7 +211,7 @@
         for half in range(2):
             ring_copy(half, way, step, k).wait_recv()
             if step < 3 or (step == 3 and way == last_way(k)):
-                go(ring_copy(half, way, step + 1, k))
+                ring_copy(half, way, step + 1, k).start()
             share(half, here(half) - step if way == 0 else here(half) + step, k)
 
     col = lax.broadcasted_iota(jnp.int32, (1, 256), 1)
@@ -240,14 +235,15 @@
         acc[:, 0:CUT] += dot(exp0[(z + NZ + OFFSETS[k]) % NZ], wg0[k].reshape(256, CUT))
 
     def finish(k):
-        for copy in core_list[k]:
-            copy.wait_recv()
+        low, high = CHUNKS[k]
+        for half, piece in enumerate((wg0.at[low:high, :, c], wg1.at[:, low:high, c])):
+            remote(piece, piece, core_send.at[half], core_recv.at[half, k], core).wait_recv()
         for slot in range(*CHUNKS[k]):
             project(slot)
 
     for half in range(2):
-        go(first_copy(half, 1))
-        go(first_copy(half, 2))
+        first_copy(half, 1).start()
+        first_copy(half, 2).start()
     for at, entry in enumerate(ROUTE):
         if entry[0] == "start":
             begin(entry[1])
@@ -255,7 +251,7 @@
             for half in range(2):
                 first_copy(half, entry[1]).wait_recv()
                 if entry[1] <= 5:
-                    go(first_copy(half, entry[1] + 2))
+                    first_copy(half, entry[1] + 2).start()
         else:
             advance(*entry)
         if at == 0:
@@ -352,7 +348,7 @@
     def a_copy(i, d):
         to_y, to_z = (y + 2 * i) % NY, (z + d) % NZ
         return remote(
-            picked.at[4 * to_z + to_y // 2], arrived.at[pair, z], a_send.at[i, d], a_recv.at[i, d], device(x, to_y, to_z, c)
+            picked.at[4 * to_z + to_y // 2], arrived.at[pair, z], a_send, a_recv, device(x, to_y, to_z, c)
         )
 
     for i, d in FAR:
@@ -382,8 +378,10 @@
             is_tail,
         )
 
-    for i, d in FAR[::-1]:
-        a_copy(i, d).wait_recv()
+    def all_of(send, recv):
+        return remote(picked.at[0:31], home.at[0:31], send, recv, core)
+
+    all_of(a_send, a_recv).wait_recv()
     left, right = unfolded(arrived[...])
     rows[par, c, :, quarter(x)] = jnp.concatenate([left, right[:, 0:128]], axis=1)
 
@@ -415,17 +413,18 @@
         q_index = (x + (0, 0, NX - 1, 1, 2)[j]) % NX
         return same(parity, q_index, low, high, yp_send.at[j], yp_recv.at[j], mate)
 
-    group_sent, to_core = [], ([], [])
+    group_sent = []
+
+    def to_core_all(main, extra, which):
+        return pieces(main, main, extra, extra, cg_send, cg_recv.at[which], core, x >= 0)
+
 
     def put(copy):
         copy.start()
         group_sent.append(copy)
 
     def over(which, q_index, low, high):
-        index = len(to_core[0]) + len(to_core[1])
-        copy = same(par if which == 0 else 1 - par, q_index, low, high, cg_send.at[index], cg_recv.at[index], core)
-        put(copy)
-        to_core[which].append(copy)
+        same(par if which == 0 else 1 - par, q_index, low, high, cg_send, cg_recv.at[which], core).start()
 
     def take_x(which, way, j):
         q_index = x_from(way, j)
@@ -475,8 +474,7 @@
     take_x(1, 1, 1)
     for load in loads[9:]:
         load.wait()
-    for copy in to_core[0]:
-        copy.wait_recv()
+    to_core_all(rows.at[:, :, :, 0:QW], rows.at[0, 0, :, 0:128], 0).wait_recv()
     expert(par, 1 - c)
     r1_copy(0).start()
     take_x(1, 0, 1)
@@ -525,8 +523,7 @@
     both_cores(par)
     for d in (2, 1, 3):
         own_sum_copy(d).start()
-    for copy in to_core[1]:
-        copy.wait_recv()
+    to_core_all(rows.at[:, :, :, 0:QW], rows.at[0, 0, :, 0:128], 1).wait_recv()
     expert(1 - par, 1 - c)
     r1_copy(1).start()
     expert(1 - par, c)
@@ -572,14 +569,13 @@
     def aa_copy(i, d):
         to_y, to_z = (y + 2 * i) % NY, (z + d) % NZ
         return remote(
-            returning.at[to_y // 2, to_z], home.at[4 * z + pair], aa_send.at[i, d], aa_recv.at[i, d], device(x, to_y, to_z, c)
+            returning.at[to_y // 2, to_z], home.at[4 * z + pair], aa_send, aa_recv, device(x, to_y, to_z, c)
         )
 
     for i, d in FAR:
         aa_copy(i, d).start()
     home[4 * z + pair] = returning[pair, z]
-    for i, d in FAR[::-1]:
-        aa_copy(i, d).wait_recv()
+    all_of(aa_send, aa_recv).wait_recv()
     left, right = unfolded(home[...])
     final[...] = (residual + jnp.concatenate([dot(placing, left), dot(placing, right)], axis=1)).astype(BF16)
 
@@ -611,9 +607,15 @@
     for h in range(2):
         for d in (1, 2, 3):
             pl.when((x + d) % NX == 0)(tail_copy(h, d).wait_send)
-    for i, d in FAR:
-        a_copy(i, d).wait_send()
-        aa_copy(i, d).wait_send()
+    all_of(a_send, a_recv).wait_send()
+    all_of(aa_send, aa_recv).wait_send()
+    for half, (strips, ringed, shared) in enumerate(
+        ((wg0.at[0:7, 0, 0], wg0.at[:, 0:7, 0], wg0.at[:, :, 0]), (wg1.at[0, 0:7, 0], wg1.at[0:7, :, 0], wg1.at[:, :, 0]))
+    ):
+        remote(strips, strips, s1_send.at[half], s1_recv.at[half, 0], core).wait_send()
+        remote(ringed, ringed, ring_send.at[half], ring_recv.at[half, 0, 0], core).wait_send()
+        remote(shared, shared, core_send.at[half], core_recv.at[half, 0], core).wait_send()
+    to_core_all(rows.at[:, :, :, 0 : 2 * QW], rows.at[0, :, :, 0:128], 0).wait_send()
     for copy in group_sent:
         copy.wait_send()
     for k in range(2):
@@ -652,12 +654,12 @@
             v(D, 512), v(512, D), v(32, 16, 256), v(4, 8, 16, 256), v(2, 2, 256, D), v(2, 2, 256, D), v(2, 256, D),
             v(2, 256, D), v(3, FIRST, QP), v(3, FIRST, QP), v(256 - FIRST, D), v(FIRST, QP), v(256 - FIRST, D), v(FIRST, QP), v(3, 256 - FIRST, QP),
             v(4, 8, 16, 256), v(32, 16, 256), v(256, QP), v(64, D),
-            sem((2, 7)), sem((2, 7)), sem((2, 2, 20)), sem((2, 2, 20)), sem((2, 40)), sem((2, 40)),
+            sem((2,)), sem((2, 7)), sem((2,)), sem((2, 2, 20)), sem((2,)), sem((2, 5)),
             sem((2, 3)), sem((2, 3)), sem((2, 3)), sem((2, 3)),
-            sem((11,)), sem((4, 8)), sem((4, 8)), sem((5, 2)), sem((5, 2)),
-            sem((2, 2, 3, 2)), sem((2, 2, 3, 2)), sem((18, 2)), sem((18, 2)),
+            sem((11,)), sem, sem, sem((5, 2)), sem((5, 2)),
+            sem((2, 2, 3, 2)), sem((2, 2, 3, 2)), sem((2,)), sem((2, 2)),
             sem((2,)), sem((2,)), sem((3, 2)), sem((3, 2)), sem((2, 3, 2)), sem((2, 3, 2)), sem, sem, sem((3, 2)), sem((3, 2)), sem((2,)), sem((2,)),
-            sem((4, 8)), sem((4, 8)), sem((3, 2)), sem((3, 2)),
+            sem, sem, sem((3, 2)), sem((3, 2)),
         ],
         compiler_params=pltpu.CompilerParams(collective_id=1, has_side_effects=True, vmem_limit_bytes=56 << 20),
     )(images, attn_gain, mlp_gain, qkv, proj_t, ids_t, gates_t, kept, counts, w_in, w_out)

time: 129 us -> 125 us (0.969)
  Pallas kernels: 127 us -> 123 us
    pallas_call x1, Pallas kernels: 127 us -> 123 us  [block(): pl.pallas_call(block_kernel, name='block', out_shape=jax.ShapeDtypeStruct...]
where the time goes in v5:
time: 125 us
  Pallas kernels  123 us (98%)
  local copies, waits for them, and re-layouts  1.63 us (1%)
    pallas_call x1, Pallas kernels, block(): pl.pallas_call(block_kernel, name='block', out_shape=jax.ShapeDtypeStruct...  123 us

profile of v5, /device:TPU:10, one launch (start us, length us, event | category | flops | bytes accessed | tf_op | source)
XLA Modules:
  0.0 124.9 jit_solution(816228001689740772)
XLA Ops:
  0.0 123.2 %block.1 = bf16[64,1664]{1,0:T(8,128)(2,1)} custom-call(bf16[256,1664]{1,0:T(8,128)(2,1)} %images_hbm.1, f32[1664]{0:T(1024)} %attn_gain_hbm.1, f32[1664]{0:T(1024)} %mlp_gain_hbm.1, bf16[3,13,416]{2,1,0:T(8,128)(2,1)} %qkv_hbm.1, bf16[13,416]{1,0:T(8,128)(2,1)} %bitcast.6, s32[2,256]{1,0:T(2,128)} %bitcast.8, bf16[2,256]{1,0:T(2,128)(2,1)} %bitcast.9, ...), custom_call_target="tpu_custom_call" | custom-call | tf_op jit(solution)/shard_map/block/pallas_call | solution.py:642
  123.2 1.6 %copy.13 = bf16[64,1664]{1,0:T(8,128)(2,1)} copy(bf16[64,1664]{1,0:T(8,128)(2,1)} %block.1) | data formatting | bytes 425984

commit v6 on v5

--- a/solution.py
+++ b/solution.py
@@ -58,13 +58,7 @@
 CUT = 896
 OFFSETS = (0, 1, -1, 2, -2, 3, -3, 4)
 CHUNKS = ((0, 1), (1, 3), (3, 5), (5, 7), (7, 8))
-ROUTE = (
-    ("start", 0), ("first", 1), ("first", 2), ("start", 1), (1, 1, 0), (0, 1, 0), ("first", 3), ("first", 4), ("start", 2),
-    (1, 1, 1), (0, 1, 1), (1, 2, 0), (0, 2, 0), ("first", 5), ("first", 6), ("start", 3), (1, 1, 2), (0, 1, 2), (1, 2, 1),
-    (0, 2, 1), (1, 3, 0), (0, 3, 0), ("first", 7), ("start", 4), (0, 1, 3), (1, 1, 3), (0, 2, 2), (1, 2, 2), (0, 3, 1),
-    (1, 3, 1), (0, 1, 4), (1, 4, 0), (1, 1, 4), (0, 2, 3), (1, 2, 3), (0, 3, 2), (0, 2, 4), (1, 3, 2), (0, 3, 3), (1, 4, 1),
-    (1, 2, 4), (0, 3, 4), (1, 3, 3), (1, 4, 2), (0, 4, 3), (1, 3, 4), (0, 4, 4),
-)
+ROUTE = (('start', 0), ('first', 1), ('first', 2), ('start', 1), (1, 1, 0), (0, 1, 0), ('first', 3), ('first', 4), ('start', 2), (1, 1, 1), (0, 1, 1), (1, 2, 0), (0, 2, 0), ('first', 5), ('first', 6), ('start', 3), (1, 1, 2), (0, 1, 2), (1, 2, 1), (0, 2, 1), (1, 3, 0), (0, 3, 0), ('first', 7), ('start', 4), (0, 1, 3), (1, 1, 3), (0, 2, 2), (1, 2, 2), (0, 3, 1), (1, 3, 1), (0, 4, 0), (0, 1, 4), (1, 1, 4), (0, 2, 3), (1, 2, 3), (0, 3, 2), (1, 3, 2), (0, 2, 4), (1, 4, 1), (1, 2, 4), (0, 3, 3), (1, 3, 3), (1, 4, 2), (0, 3, 4), (1, 3, 4), (0, 4, 3), (0, 4, 4))
 
 
 def slot_offset(s):
@@ -205,7 +199,7 @@
             share(half, here(half), k)
 
     def last_way(k):
-        return 1 if k < 3 else 0
+        return 1 if k in (1, 2) else 0
 
     def advance(way, step, k):
         for half in range(2):
@@ -264,10 +258,8 @@
             normed = (center * lax.rsqrt(spread + 1e-06) * attn_gain[...].reshape(1, D)).astype(BF16)
         if 8 <= at < 24 and at % 2 == 0:
             expand((at - 8) // 2)
-        if at in (38, 42, 45):
-            finish((38, 42, 45).index(at))
-    finish(3)
-    finish(4)
+    for k in range(5):
+        finish(k)
     for k in range(8):
         part = dot(exp1[k], wg1[k].reshape(256, D - CUT)[:, 0 : 1280 - CUT])
         late = part if k == 0 else late + part

time: 125 us -> 126 us (level)
  no operation moved by 1% of the time
where the time goes in v6:
time: 126 us
  Pallas kernels  124 us (98%)
  local copies, waits for them, and re-layouts  1.63 us (1%)
    pallas_call x1, Pallas kernels, block(): pl.pallas_call(block_kernel, name='block', out_shape=jax.ShapeDtypeStruct...  124 us

profile of v6, /device:TPU:10, one launch (start us, length us, event | category | flops | bytes accessed | tf_op | source)
XLA Modules:
  0.0 126.1 jit_solution(11266245367062675854)
XLA Ops:
  0.0 124.4 %block.1 = bf16[64,1664]{1,0:T(8,128)(2,1)} custom-call(bf16[256,1664]{1,0:T(8,128)(2,1)} %images_hbm.1, f32[1664]{0:T(1024)} %attn_gain_hbm.1, f32[1664]{0:T(1024)} %mlp_gain_hbm.1, bf16[3,13,416]{2,1,0:T(8,128)(2,1)} %qkv_hbm.1, bf16[13,416]{1,0:T(8,128)(2,1)} %bitcast.6, s32[2,256]{1,0:T(2,128)} %bitcast.8, bf16[2,256]{1,0:T(2,128)(2,1)} %bitcast.9, ...), custom_call_target="tpu_custom_call" | custom-call | tf_op jit(solution)/shard_map/block/pallas_call | solution.py:634
  124.4 1.6 %copy.13 = bf16[64,1664]{1,0:T(8,128)(2,1)} copy(bf16[64,1664]{1,0:T(8,128)(2,1)} %block.1) | data formatting | bytes 425984
